TPU v7x, 128 devices: a whole 4x4x4 slice. The times are simulated.
128 devices in a mesh: grp: 2 (over z_hi), ctx: 16 (over x, y), head: 4 (over z_lo, core).
Axes of the slice: x: 4, y: 4, z: 4 (z_hi: 2, z_lo: 2; z = z_hi * 2 + z_lo), core: 2. Of those that a mesh axis runs over, the one named last changes fastest.
Arguments:
- queries: bfloat16 [4, 2048, 5120], P('grp', 'ctx', 'head'), may hold values from -32 to 32
- keys: bfloat16 [4, 2048, 1024], P('grp', 'ctx', 'head'), may hold values from -6 to 6
- values: bfloat16 [4, 2048, 1024], P('grp', 'ctx', 'head'), may hold values from -6 to 6
- prefix_keys: bfloat16 [4096, 1024], P(('grp', 'ctx'), 'head'), may hold values from -16 to 16
- shared_prompt_values: bfloat16 [4096, 1024], P(('grp', 'ctx'), 'head'), may hold values from -6 to 6
- lengths: int32 [4], P('grp'), may hold values from 512 to 2048, as said below
- grad_out: bfloat16 [4, 2048, 5120], P('grp', 'ctx', 'head'), may hold values from -6 to 6
Outputs:
- attended: bfloat16 [4, 2048, 5120], P('grp', 'ctx', 'head')
- query_grad: bfloat16 [4, 2048, 5120], P('grp', 'ctx', 'head')
- key_grad: bfloat16 [4, 2048, 1024], P('grp', 'ctx', 'head')
- value_grad: bfloat16 [4, 2048, 1024], P('grp', 'ctx', 'head')
- prefix_key_grad: bfloat16 [4096, 1024], P(('grp', 'ctx'), 'head')
- prefix_value_grad: bfloat16 [4096, 1024], P(('grp', 'ctx'), 'head')
Inputs may be any that keep to these rules, and one draw needn't show every extreme that they name: `lengths`: one response has exactly 2048 live positions and another exactly 512.
All inputs are finite; a program needn't handle non-finite values.
Results may differ from a plain program's by a relative error of at most 0.04.
Values may be sent and summed in bfloat16 or wider, within the bound.
A program may use at most 192 MiB of HBM per device.

v0:
```python
import math

import jax
import jax.numpy as jnp
from jax import lax
from jax.sharding import PartitionSpec as P

HEAD_SIZE = 128


def shards(queries, keys, values, prefix_keys, shared_prompt_values, lengths, grad_out):
    resp_local, tdev, qwidth = queries.shape
    kwidth = keys.shape[2]
    kv_dev = kwidth // HEAD_SIZE
    head_groups = qwidth // kwidth
    scale = 1.0 / math.sqrt(HEAD_SIZE)
    full_len = tdev * lax.axis_size("ctx")
    prompt_keys, prompt_values = (
        lax.all_gather(prefix_keys, ("grp", "ctx"), axis=0, tiled=True),
        lax.all_gather(shared_prompt_values, ("grp", "ctx"), axis=0, tiled=True),
    )
    resp_k, resp_v = (
        lax.all_gather(keys, "ctx", axis=1, tiled=True),
        lax.all_gather(values, "ctx", axis=1, tiled=True),
    )
    pcount = prompt_keys.shape[0]
    unique_count = pcount + full_len
    joined_keys = jnp.concatenate(
        [jnp.broadcast_to(prompt_keys[None], (resp_local, pcount, kwidth)), resp_k], 1
    ).reshape(resp_local, unique_count, kv_dev, HEAD_SIZE)
    joined_values = jnp.concatenate(
        [jnp.broadcast_to(prompt_values[None], (resp_local, pcount, kwidth)), resp_v], 1
    ).reshape(resp_local, unique_count, kv_dev, HEAD_SIZE)
    first = lax.axis_index("ctx") * tdev
    tpos = first + jnp.arange(tdev, dtype=jnp.int32)
    upos = jnp.arange(unique_count, dtype=jnp.int32) - pcount
    valid = tpos[None, :] < lengths[:, None]
    mask = (upos[None, None, :] < 0) | (upos[None, None, :] <= tpos[None, :, None]) & (
        upos[None, None, :] < lengths[:, None, None]
    )
    glive = jnp.where(valid[:, :, None], grad_out, jnp.zeros_like(grad_out))
    qsplit = jnp.moveaxis(queries.reshape(resp_local, tdev, kv_dev, head_groups, HEAD_SIZE), 3, 0)
    gsplit = jnp.moveaxis(glive.reshape(resp_local, tdev, kv_dev, head_groups, HEAD_SIZE), 3, 0)

    def step(carry, xs):
        key_gradient, value_gradient = carry
        qgroup, ggroup = xs
        scores = (
            jnp.einsum("rtkd,rukd->rktu", qgroup, joined_keys, preferred_element_type=jnp.float32)
            * scale
        )
        scores = jnp.where(mask[:, None], scores, -jnp.inf)
        top = jnp.max(scores, -1, keepdims=True)
        lse = top + jnp.log(jnp.sum(jnp.exp(scores - top), -1, keepdims=True))
        probs = jnp.exp(scores - lse)
        plow = probs.astype(jnp.bfloat16)
        outrow = jnp.einsum(
            "rktu,rukd->rtkd", plow, joined_values, preferred_element_type=jnp.float32
        )
        outlow = jnp.where(valid[:, :, None, None], outrow, 0.0).astype(jnp.bfloat16)
        delta = jnp.sum(ggroup.astype(jnp.float32) * outlow.astype(jnp.float32), -1)
        dprobs = jnp.einsum(
            "rtkd,rukd->rktu", ggroup, joined_values, preferred_element_type=jnp.float32
        )
        dscores = (probs * (dprobs - jnp.transpose(delta, (0, 2, 1))[..., None]) * scale).astype(
            jnp.bfloat16
        )
        dquery = jnp.einsum(
            "rktu,rukd->rtkd", dscores, joined_keys, preferred_element_type=jnp.float32
        ).astype(jnp.bfloat16)
        key_gradient = key_gradient + jnp.einsum(
            "rktu,rtkd->rukd", dscores, qgroup, preferred_element_type=jnp.float32
        )
        value_gradient = value_gradient + jnp.einsum(
            "rktu,rtkd->rukd", plow, ggroup, preferred_element_type=jnp.float32
        )
        return ((key_gradient, value_gradient), (outlow, dquery, lse[..., 0], delta))

    zero_fill = jnp.zeros((resp_local, unique_count, kv_dev, HEAD_SIZE), jnp.float32)
    (key_gradient, value_gradient), (outs, dqs, lses, deltas) = lax.scan(
        step, (zero_fill, zero_fill), (qsplit, gsplit)
    )
    attended = jnp.transpose(outs, (1, 2, 3, 0, 4)).reshape(resp_local, tdev, qwidth)
    query_grad = jnp.transpose(dqs, (1, 2, 3, 0, 4)).reshape(resp_local, tdev, qwidth)
    pk_part = jnp.sum(key_gradient[:, :pcount], 0).reshape(pcount, kwidth)
    pv_part = jnp.sum(value_gradient[:, :pcount], 0).reshape(pcount, kwidth)
    pk_sum, pv_sum = (
        lax.psum_scatter(pk_part, ("grp", "ctx"), scatter_dimension=0, tiled=True),
        lax.psum_scatter(pv_part, ("grp", "ctx"), scatter_dimension=0, tiled=True),
    )
    rk_part = key_gradient[:, pcount:].reshape(resp_local, full_len, kwidth)
    rv_part = value_gradient[:, pcount:].reshape(resp_local, full_len, kwidth)
    rk_sum, rv_sum = (
        lax.psum_scatter(
            rk_part.astype(jnp.bfloat16), "ctx", scatter_dimension=1, tiled=True
        ).astype(jnp.float32),
        lax.psum_scatter(
            rv_part.astype(jnp.bfloat16), "ctx", scatter_dimension=1, tiled=True
        ).astype(jnp.float32),
    )
    key_grad = rk_sum.astype(jnp.bfloat16)
    value_grad = rv_sum.astype(jnp.bfloat16)
    return (
        attended,
        query_grad,
        key_grad,
        value_grad,
        pk_sum.astype(jnp.bfloat16),
        pv_sum.astype(jnp.bfloat16),
    )


def solution(mesh):
    return jax.shard_map(
        shards,
        mesh=mesh,
        in_specs=(
            P("grp", "ctx", "head"),
            P("grp", "ctx", "head"),
            P("grp", "ctx", "head"),
            P(("grp", "ctx"), "head"),
            P(("grp", "ctx"), "head"),
            P("grp"),
            P("grp", "ctx", "head"),
        ),
        out_specs=(
            P("grp", "ctx", "head"),
            P("grp", "ctx", "head"),
            P("grp", "ctx", "head"),
            P("grp", "ctx", "head"),
            P(("grp", "ctx"), "head"),
            P(("grp", "ctx"), "head"),
        ),
        check_vma=False,
    )
```

profile of v0, /device:TPU:0, one launch (start us, length us, event | category | flops | bytes accessed | tf_op | source)
XLA Modules:
  0.0 1136.8 jit_solution(15607220444153494929)
XLA Ops:
  16.8 40.6 %all-gather.11.cloned.1.call-done = bf16[2,2048,256]{2,1,0:T(8,128)(2,1)} async-done(((bf16[2,128,256]{2,1,0:T(8,128)(2,1)}), bf16[2,2048,256]{2,1,0:T(8,128)(2,1)}) %all-gather.11.cloned.1.call-update) | async-done | bytes 2097168 | tf_op jit(solution)/shard_map/all_gather | solution.py:24
  61.5 70.8 %all-gather.5.cloned.1.call-done = bf16[4096,256]{1,0:T(8,128)(2,1)} async-done(((bf16[128,256]{1,0:T(8,128)(2,1)}), bf16[4096,256]{1,0:T(8,128)(2,1)}) %all-gather.5.cloned.1.call-update) | async-done | bytes 2097168 | tf_op jit(solution)/shard_map/all_gather | solution.py:19
  136.4 43.0 %all-gather.7.cloned.1.call-done = bf16[2,2048,256]{1,2,0:T(8,128)(2,1)} async-done(((bf16[2,128,256]{1,2,0:T(8,128)(2,1)}), bf16[2,2048,256]{1,2,0:T(8,128)(2,1)}) %all-gather.7.cloned.1.call-update) | async-done | bytes 2097168 | tf_op jit(solution)/shard_map/all_gather | solution.py:23
  193.7 60.3 %all-gather.9.cloned.1.call-done = bf16[4096,256]{1,0:T(8,128)(2,1)} async-done(((bf16[128,256]{1,0:T(8,128)(2,1)}), bf16[4096,256]{1,0:T(8,128)(2,1)}) %all-gather.9.cloned.1.call-update) | async-done | bytes 2097168 | tf_op jit(solution)/shard_map/all_gather | solution.py:20
  265.2 319.5 %while.17 = (s32[]{:T(128)}, f32[2,6144,2,128]{1,3,2,0:T(8,128)}, f32[2,6144,2,128]{1,3,2,0:T(8,128)}, bf16[5,2,128,2,128]{2,4,0,3,1:T(8,128)(2,1)}, bf16[5,2,12...) while((s32[]{:T(128)}, f32[2,6144,2,128]{1,3,2,0:T(8,128)}, ...), condition=%wide.region_4.5_spmd.clone, body=%wide.region_0.4_spmd.clone.sunk | while | flops 4892064768 | bytes 258123568 | solution.py:80
  276.9 12.4 %bitcast_add_fusion.5 = f32[2,6144,2,128]{1,3,2,0:T(8,128)} fusion(f32[2,6144,2,128]{1,3,2,0:T(8,128)} %get-tuple-element.315, pred[]{:T(512)S(6)} %compare.3, f32[2,2,128,6144]{3,2,1,0:T(8,128)} %copy-done, f32[2,2,128]{2,1,0:T(2,128)S(1)} %log_add_fusion.2, bf16[1,2,128,2,128]{2,4,0,3,1:T(8,128)(2,1)S(1)} %constant_dynamic-slice_fusion.2), kind=kOutput, calls=%fused_computation.2.clone.1 | convolution fusion | flops 817889280 | bytes 37881856 | tf_op jit(solution)/shard_map/while/body/eval_jaxpr/rktu,rtkd->rukd/dot_general | solution.py:74
  298.2 10.5 multiply_convert_fusion.2
  335.0 16.0 %bitcast_add_fusion.5 = f32[2,6144,2,128]{1,3,2,0:T(8,128)} fusion(f32[2,6144,2,128]{1,3,2,0:T(8,128)} %get-tuple-element.315, pred[]{:T(512)S(6)} %compare.3, f32[2,2,128,6144]{3,2,1,0:T(8,128)} %copy-done, f32[2,2,128]{2,1,0:T(2,128)S(1)} %log_add_fusion.2, bf16[1,2,128,2,128]{2,4,0,3,1:T(8,128)(2,1)S(1)} %constant_dynamic-slice_fusion.2), kind=kOutput, calls=%fused_computation.2.clone.1 | convolution fusion | flops 817889280 | bytes 37881856 | tf_op jit(solution)/shard_map/while/body/eval_jaxpr/rktu,rtkd->rukd/dot_general | solution.py:74
  359.9 10.5 multiply_convert_fusion.2
  375.9 12.7 %bitcast_add_fusion.4 = f32[2,6144,2,128]{1,3,2,0:T(8,128)} fusion(f32[2,6144,2,128]{1,3,2,0:T(8,128)} %get-tuple-element.314, bf16[2,2,128,6144]{3,2,1,0:T(8,128)(2,1)} %copy-done.1, pred[]{:T(512)S(6)} %compare.3, bf16[5,2,128,2,128]{2,4,0,3,1:T(8,128)(2,1)S(1)} %get-tuple-element.334, s32[]{:T(128)} %get-tuple-element.313), kind=kOutput, calls=%fused_computation.3.clone.1 | convolution fusion | flops 811597824 | bytes 31588356 | tf_op jit(solution)/shard_map/while/body/eval_jaxpr/rktu,rtkd->rukd/dot_general | solution.py:71
  400.4 16.0 %bitcast_add_fusion.5 = f32[2,6144,2,128]{1,3,2,0:T(8,128)} fusion(f32[2,6144,2,128]{1,3,2,0:T(8,128)} %get-tuple-element.315, pred[]{:T(512)S(6)} %compare.3, f32[2,2,128,6144]{3,2,1,0:T(8,128)} %copy-done, f32[2,2,128]{2,1,0:T(2,128)S(1)} %log_add_fusion.2, bf16[1,2,128,2,128]{2,4,0,3,1:T(8,128)(2,1)S(1)} %constant_dynamic-slice_fusion.2), kind=kOutput, calls=%fused_computation.2.clone.1 | convolution fusion | flops 817889280 | bytes 37881856 | tf_op jit(solution)/shard_map/while/body/eval_jaxpr/rktu,rtkd->rukd/dot_general | solution.py:74
  425.3 10.5 multiply_convert_fusion.2
  441.3 12.7 %bitcast_add_fusion.4 = f32[2,6144,2,128]{1,3,2,0:T(8,128)} fusion(f32[2,6144,2,128]{1,3,2,0:T(8,128)} %get-tuple-element.314, bf16[2,2,128,6144]{3,2,1,0:T(8,128)(2,1)} %copy-done.1, pred[]{:T(512)S(6)} %compare.3, bf16[5,2,128,2,128]{2,4,0,3,1:T(8,128)(2,1)S(1)} %get-tuple-element.334, s32[]{:T(128)} %get-tuple-element.313), kind=kOutput, calls=%fused_computation.3.clone.1 | convolution fusion | flops 811597824 | bytes 31588356 | tf_op jit(solution)/shard_map/while/body/eval_jaxpr/rktu,rtkd->rukd/dot_general | solution.py:71
  465.7 16.0 %bitcast_add_fusion.5 = f32[2,6144,2,128]{1,3,2,0:T(8,128)} fusion(f32[2,6144,2,128]{1,3,2,0:T(8,128)} %get-tuple-element.315, pred[]{:T(512)S(6)} %compare.3, f32[2,2,128,6144]{3,2,1,0:T(8,128)} %copy-done, f32[2,2,128]{2,1,0:T(2,128)S(1)} %log_add_fusion.2, bf16[1,2,128,2,128]{2,4,0,3,1:T(8,128)(2,1)S(1)} %constant_dynamic-slice_fusion.2), kind=kOutput, calls=%fused_computation.2.clone.1 | convolution fusion | flops 817889280 | bytes 37881856 | tf_op jit(solution)/shard_map/while/body/eval_jaxpr/rktu,rtkd->rukd/dot_general | solution.py:74
  490.6 10.5 multiply_convert_fusion.2
  506.6 12.7 %bitcast_add_fusion.4 = f32[2,6144,2,128]{1,3,2,0:T(8,128)} fusion(f32[2,6144,2,128]{1,3,2,0:T(8,128)} %get-tuple-element.314, bf16[2,2,128,6144]{3,2,1,0:T(8,128)(2,1)} %copy-done.1, pred[]{:T(512)S(6)} %compare.3, bf16[5,2,128,2,128]{2,4,0,3,1:T(8,128)(2,1)S(1)} %get-tuple-element.334, s32[]{:T(128)} %get-tuple-element.313), kind=kOutput, calls=%fused_computation.3.clone.1 | convolution fusion | flops 811597824 | bytes 31588356 | tf_op jit(solution)/shard_map/while/body/eval_jaxpr/rktu,rtkd->rukd/dot_general | solution.py:71
  531.0 16.0 %bitcast_add_fusion.5 = f32[2,6144,2,128]{1,3,2,0:T(8,128)} fusion(f32[2,6144,2,128]{1,3,2,0:T(8,128)} %get-tuple-element.315, pred[]{:T(512)S(6)} %compare.3, f32[2,2,128,6144]{3,2,1,0:T(8,128)} %copy-done, f32[2,2,128]{2,1,0:T(2,128)S(1)} %log_add_fusion.2, bf16[1,2,128,2,128]{2,4,0,3,1:T(8,128)(2,1)S(1)} %constant_dynamic-slice_fusion.2), kind=kOutput, calls=%fused_computation.2.clone.1 | convolution fusion | flops 817889280 | bytes 37881856 | tf_op jit(solution)/shard_map/while/body/eval_jaxpr/rktu,rtkd->rukd/dot_general | solution.py:74
  555.9 10.5 multiply_convert_fusion.2
  571.9 12.7 %bitcast_add_fusion.4 = f32[2,6144,2,128]{1,3,2,0:T(8,128)} fusion(f32[2,6144,2,128]{1,3,2,0:T(8,128)} %get-tuple-element.314, bf16[2,2,128,6144]{3,2,1,0:T(8,128)(2,1)} %copy-done.1, pred[]{:T(512)S(6)} %compare.3, bf16[5,2,128,2,128]{2,4,0,3,1:T(8,128)(2,1)S(1)} %get-tuple-element.334, s32[]{:T(128)} %get-tuple-element.313), kind=kOutput, calls=%fused_computation.3.clone.1 | convolution fusion | flops 811597824 | bytes 31588356 | tf_op jit(solution)/shard_map/while/body/eval_jaxpr/rktu,rtkd->rukd/dot_general | solution.py:71
  584.7 10.4 slice_reduce_fusion
  618.9 171.2 %reduce-scatter.9.cloned.1.call-done = f32[128,256]{1,0:T(8,128)} async-done(((f32[4096,256]{1,0:T(8,128)}), f32[128,256]{1,0:T(8,128)}) %reduce-scatter.9.cloned.1.call-update) | async-done | bytes 131088 | tf_op jit(solution)/shard_map/reduce_scatter | solution.py:88
  791.7 187.7 %reduce-scatter.11.cloned.1.call-done = f32[128,256]{1,0:T(8,128)} async-done(((f32[4096,256]{1,0:T(8,128)}), f32[128,256]{1,0:T(8,128)}) %reduce-scatter.11.cloned.1.call-update) | async-done | bytes 131088 | tf_op jit(solution)/shard_map/reduce_scatter | solution.py:89
  980.9 71.3 %reduce-scatter.5.cloned.1.call-done = bf16[2,128,256]{2,1,0:T(8,128)(2,1)} async-done(((bf16[2,2048,256]{2,1,0:T(8,128)(2,1)}), bf16[2,128,256]{2,1,0:T(8,128)(2,1)}) %reduce-scatter.5.cloned.1.call-update) | async-done | bytes 131088 | tf_op jit(solution)/shard_map/reduce_scatter | solution.py:94
  1052.2 77.8 %reduce-scatter.7.cloned.1.call-done = bf16[2,128,256]{2,1,0:T(8,128)(2,1)} async-done(((bf16[2,2048,256]{2,1,0:T(8,128)(2,1)}), bf16[2,128,256]{2,1,0:T(8,128)(2,1)}) %reduce-scatter.7.cloned.1.call-update) | async-done | bytes 131088 | tf_op jit(solution)/shard_map/reduce_scatter | solution.py:97
  (162 shorter events, 209.4 us)
Async XLA Ops:
  7.2 50.3 %all-gather.11.cloned.1.call-start = ((), (), s32[]{:S(2)}) async-start(), calls=%async_computation.7 | async-start | bytes 2228224 | tf_op jit(solution)/shard_map/all_gather | solution.py:24
  7.9 124.4 %all-gather.5.cloned.1.call-start = ((), (), s32[]{:S(2)}) async-start(), calls=%async_computation.4 | async-start | bytes 2162688 | tf_op jit(solution)/shard_map/all_gather | solution.py:19
  8.6 170.7 %all-gather.7.cloned.1.call-start = ((), (), s32[]{:S(2)}) async-start(), calls=%async_computation.5 | async-start | bytes 2228224 | tf_op jit(solution)/shard_map/all_gather | solution.py:23
  10.4 243.7 %all-gather.9.cloned.1.call-start = ((), (), s32[]{:S(2)}) async-start(), calls=%async_computation.6 | async-start | bytes 2162688 | tf_op jit(solution)/shard_map/all_gather | solution.py:20
  11.0 779.2 %reduce-scatter.9.cloned.1.call-start = ((), (), s32[]{:S(2)}) async-start(), calls=%async_computation.10 | async-start | bytes 4325376 | tf_op jit(solution)/shard_map/reduce_scatter | solution.py:88
  260.3 5.0 copy-start.5
  271.4 4.6 copy-start
  289.5 21.9 %slice-start = ((s8[6291456]{0:T(1024)(128)(4,1)}), s8[2097152]{0:T(1024)(128)(4,1)S(1)}, s32[]{:S(2)}) async-start(s8[6291456]{0:T(1024)(128)(4,1)} %bitcast.88), calls=%async_computation.12 | async-start | bytes 4194304 | tf_op jit(solution)/shard_map/while
  298.2 13.2 %slice-start.1 = ((s8[6291456]{0:T(1024)(128)(4,1)}), s8[4194304]{0:T(1024)(128)(4,1)S(1)}, s32[]{:S(2)}) async-start(s8[6291456]{0:T(1024)(128)(4,1)} %bitcast.88), calls=%async_computation.13 | async-start | bytes 8388608 | tf_op jit(solution)/shard_map/while
  329.5 4.6 copy-start
  351.2 21.9 %slice-start = ((s8[6291456]{0:T(1024)(128)(4,1)}), s8[2097152]{0:T(1024)(128)(4,1)S(1)}, s32[]{:S(2)}) async-start(s8[6291456]{0:T(1024)(128)(4,1)} %bitcast.88), calls=%async_computation.12 | async-start | bytes 4194304 | tf_op jit(solution)/shard_map/while
  359.9 13.2 %slice-start.1 = ((s8[6291456]{0:T(1024)(128)(4,1)}), s8[4194304]{0:T(1024)(128)(4,1)S(1)}, s32[]{:S(2)}) async-start(s8[6291456]{0:T(1024)(128)(4,1)} %bitcast.88), calls=%async_computation.13 | async-start | bytes 8388608 | tf_op jit(solution)/shard_map/while
  416.6 21.9 %slice-start = ((s8[6291456]{0:T(1024)(128)(4,1)}), s8[2097152]{0:T(1024)(128)(4,1)S(1)}, s32[]{:S(2)}) async-start(s8[6291456]{0:T(1024)(128)(4,1)} %bitcast.88), calls=%async_computation.12 | async-start | bytes 4194304 | tf_op jit(solution)/shard_map/while
  425.3 13.2 %slice-start.1 = ((s8[6291456]{0:T(1024)(128)(4,1)}), s8[4194304]{0:T(1024)(128)(4,1)S(1)}, s32[]{:S(2)}) async-start(s8[6291456]{0:T(1024)(128)(4,1)} %bitcast.88), calls=%async_computation.13 | async-start | bytes 8388608 | tf_op jit(solution)/shard_map/while
  460.2 4.6 copy-start
  481.9 21.9 %slice-start = ((s8[6291456]{0:T(1024)(128)(4,1)}), s8[2097152]{0:T(1024)(128)(4,1)S(1)}, s32[]{:S(2)}) async-start(s8[6291456]{0:T(1024)(128)(4,1)} %bitcast.88), calls=%async_computation.12 | async-start | bytes 4194304 | tf_op jit(solution)/shard_map/while
  490.6 13.2 %slice-start.1 = ((s8[6291456]{0:T(1024)(128)(4,1)}), s8[4194304]{0:T(1024)(128)(4,1)S(1)}, s32[]{:S(2)}) async-start(s8[6291456]{0:T(1024)(128)(4,1)} %bitcast.88), calls=%async_computation.13 | async-start | bytes 8388608 | tf_op jit(solution)/shard_map/while
  547.2 21.9 %slice-start = ((s8[6291456]{0:T(1024)(128)(4,1)}), s8[2097152]{0:T(1024)(128)(4,1)S(1)}, s32[]{:S(2)}) async-start(s8[6291456]{0:T(1024)(128)(4,1)} %bitcast.88), calls=%async_computation.12 | async-start | bytes 4194304 | tf_op jit(solution)/shard_map/while
  555.9 13.2 %slice-start.1 = ((s8[6291456]{0:T(1024)(128)(4,1)}), s8[4194304]{0:T(1024)(128)(4,1)S(1)}, s32[]{:S(2)}) async-start(s8[6291456]{0:T(1024)(128)(4,1)} %bitcast.88), calls=%async_computation.13 | async-start | bytes 8388608 | tf_op jit(solution)/shard_map/while
  600.7 378.7 %reduce-scatter.11.cloned.1.call-start = ((), (), s32[]{:S(2)}) async-start(), calls=%async_computation.11 | async-start | bytes 4325376 | tf_op jit(solution)/shard_map/reduce_scatter | solution.py:89
  606.4 445.8 %reduce-scatter.5.cloned.1.call-start = ((), (), s32[]{:S(2)}) async-start(), calls=%async_computation.8 | async-start | bytes 2228224 | tf_op jit(solution)/shard_map/reduce_scatter | solution.py:94
  611.5 5.2 copy-start.3
  611.5 6.3 copy-start.4
  611.5 518.4 %reduce-scatter.7.cloned.1.call-start = ((), (), s32[]{:S(2)}) async-start(), calls=%async_computation.9 | async-start | bytes 2228224 | tf_op jit(solution)/shard_map/reduce_scatter | solution.py:97
  (8 other events, 24.9 us)
Sparse Core Ops, SparseCore 0:
  10.2 47.2 all-gather.10
  60.6 71.6 all-gather.4
  135.0 44.3 all-gather.6
  182.3 71.6 all-gather.8
  600.8 189.2 reduce-scatter.8
  792.4 186.9 reduce-scatter.10
  983.2 68.9 reduce-scatter.4
  1056.4 73.5 reduce-scatter.6
where the time goes:
time: 1140 us
  waiting for transfers between devices  725 us (64%)
  matrix products  267 us (23%)
  local copies, waits for them, and re-layouts  90.5 us (8%)
  other arithmetic  39.9 us (4%)
  between operations  14.3 us (1%)
    reduce_scatter x1, waiting for transfers between devices, shards(): lax.psum_scatter(pv_part, ('grp', 'ctx'), scatter_dimension=0, tiled=True)  188 us
    reduce_scatter x1, waiting for transfers between devices, shards(): lax.psum_scatter(pk_part, ('grp', 'ctx'), scatter_dimension=0, tiled=True)  171 us
    reduce_scatter x1, waiting for transfers between devices, shards(): lax.psum_scatter(rv_part.astype(jnp.bfloat16), 'ctx', scatter_dimension=1...  77.8 us
    dot_general x5, matrix products, step(): jnp.einsum('rktu,rtkd->rukd', plow, ggroup, preferred_element_type=jnp.fl...  76.3 us
    reduce_scatter x1, waiting for transfers between devices, shards(): lax.psum_scatter(rk_part.astype(jnp.bfloat16), 'ctx', scatter_dimension=1...  71.3 us
    all_gather x1, waiting for transfers between devices, shards(): lax.all_gather(prefix_keys, ('grp', 'ctx'), axis=0, tiled=True)  70.8 us
    all_gather x1, waiting for transfers between devices, shards(): lax.all_gather(shared_prompt_values, ('grp', 'ctx'), axis=0, tiled=True)  60.3 us
    dot_general x5, matrix products, step(): jnp.einsum('rktu,rtkd->rukd', dscores, qgroup, preferred_element_type=jnp...  60.1 us
  transfers between devices with their start and end apart: 8, of which 8 were waited for; matrix products, arithmetic and copies ran while one was open for 4% of the time, Pallas kernels for 0%

commit v1 on v0

v1 whole, which is shorter than its diff:
```python
import functools
import math

import jax
import jax.numpy as jnp
from jax import lax
from jax.experimental import pallas as pl
from jax.experimental.pallas import tpu as pltpu
from jax.sharding import PartitionSpec as P

MESH = pl.DeviceIdType.MESH
F32, BF = jnp.float32, jnp.bfloat16
T = 128
CH = 512
HEADS = 5
R = HEADS * T
PC = 8
NT = (((1,), (1,)), ((), ()))
NN = (((1,), (0,)), ((), ()))
dot = functools.partial(lax.dot_general, preferred_element_type=F32)
N_SEM = 64


def mult(v, n):
    return pl.multiple_of(v, n)


def kernel(
    lens_ref, queries, keys, values, pkeys, pvalues, gout,
    attended, query_grad, key_grad, value_grad, pk_grad, pv_grad,
    q_ref, g_ref, kv, rbuf, pbuf, o_ref, dq_ref,
    ka, va, qa, ga, gt, gs, s_ref, e_ref, mrun, stat, turned, top_ref, acc,
    send, recv, lsem,
):
    grp, ctx, head = lax.axis_index("grp"), lax.axis_index("ctx"), lax.axis_index("head")
    x, y = ctx // 4, ctx % 4
    resp, kvh = x // 2, x % 2
    c2 = 1.4426950408889634 / math.sqrt(T)
    scale = 1.0 / math.sqrt(T)

    def xdev(d, other=0):
        return ((grp + other) % 2, ((x + d) % 4) * 4 + y, head)

    def ydev(d):
        return (grp, x * 4 + (y + d) % 4, head)

    counter = [0, 0]

    def remote(src, dst, dev):
        k = counter[0]
        counter[0] += 1
        return pltpu.make_async_remote_copy(
            src_ref=src, dst_ref=dst, send_sem=send.at[k], recv_sem=recv.at[k],
            device_id=dev, device_id_type=MESH,
        )

    def local(src, dst):
        k = counter[1]
        counter[1] += 1
        return pltpu.make_async_copy(src, dst, lsem.at[k])

    partners = [xdev(d) for d in (1, 2, 3)] + [ydev(d) for d in (1, 2, 3)] + [xdev(d, 1) for d in range(4)]
    barrier = pltpu.get_barrier_semaphore()
    for dev in partners:
        pl.semaphore_signal(barrier, inc=1, device_id=dev, device_id_type=MESH)
    pl.semaphore_wait(barrier, len(partners))

    def hd(j):
        return pl.ds(mult(j * T, T), T)

    def wide(j):
        return pl.ds(mult(j * R, T), R)

    def blk(b):
        return pl.ds(mult(b * T, T), T)

    pre, late = [], []
    for other in (1, 0):
        for d in range(4):
            tx = (x + d) % 4
            j = tx % 2
            copy = local if (d == 0 and not other) else functools.partial(remote, dev=xdev(d, other))
            for which, ref in ((0, pkeys), (1, pvalues)):
                pre.append(copy(ref.at[:, hd(j)], kv.at[y, which, blk(grp * 4 + x), :]))
    for d in range(4):
        tx = (x + d) % 4
        r, j = tx // 2, tx % 2
        copy = local if d == 0 else functools.partial(remote, dev=xdev(d))
        for which, ref in ((0, keys), (1, values)):
            pre.append(copy(ref.at[r, :, hd(j)], kv.at[y, which, blk(8 + x), :]))
        for ref, buf in ((queries, q_ref), (gout, g_ref)):
            late.append(copy(ref.at[r, :, wide(j)], buf.at[x]))
    for copy in pre + late:
        copy.start()
    for copy in pre:
        copy.wait()

    ygather = {}
    for d in (2, 1, 3):
        ygather[d] = [
            remote(kv.at[y, :, pl.ds(0, 1024), :], kv.at[y, :, pl.ds(0, 1024), :], ydev(d)),
            remote(kv.at[y, :, pl.ds(1024, 512), :], kv.at[y, :, pl.ds(1024, 512), :], ydev(d)),
        ]
        for copy in ygather[d]:
            copy.start()
    for copy in late:
        copy.wait()

    def place(d):
        sy = (y - d) % 4
        ps = pl.ds(d * 1024, 1024)
        ka[ps, :T] = kv[sy, 0, :1024, :]
        ka[ps, T:] = kv[sy, 0, :1024, :]
        va[ps, :T] = kv[sy, 1, :1024, :]
        va[ps, T:] = jnp.ones((1024, T), BF)
        for i in range(4):
            rs = pl.ds(mult(4096 + i * CH + sy * T, T), T)
            src = slice(1024 + i * T, 1024 + (i + 1) * T)
            ka[rs, :T] = kv[sy, 0, src, :]
            ka[rs, T:] = kv[sy, 0, src, :]
            va[rs, :T] = kv[sy, 1, src, :]
            va[rs, T:] = jnp.ones((T, T), BF)

    def off(i):
        return PC * i + (i * (i + 1)) // 2

    def chunk_rows(c):
        return pl.ds(mult(c * CH, CH), CH)

    def fold(s):
        return functools.reduce(jnp.maximum, [s[:, k * T:(k + 1) * T] for k in range(CH // T)])

    lane = lax.broadcasted_iota(jnp.int32, (R, T), 1)

    def prepare(i, _):
        for h in range(HEADS):
            rs = slice(h * T, (h + 1) * T)
            qs = q_ref[i, :, rs].astype(F32) * c2
            hi = qs.astype(BF)
            qa[i, rs, :T] = hi
            qa[i, rs, T:] = (qs - hi.astype(F32)).astype(BF)
        acc[i] = jnp.zeros((R, 2 * T), F32)
        mrun[i] = jnp.full((R, T), -jnp.inf, F32)
        stat[i] = jnp.zeros((R, T), F32)
        return 0

    lax.fori_loop(0, 4, prepare, 0)

    def scores(i, c, slot):
        s = dot(qa[i], ka[chunk_rows(c), :], NT)
        s_ref[slot] = s
        return fold(s)

    def weigh(i, base, count, g, top):
        old = mrun[i]
        new = jnp.maximum(old, jnp.broadcast_to(jnp.max(top, 1, keepdims=True), (R, T)))
        mrun[i] = new
        stat[i] = jnp.where(lane == g, new, stat[i])
        fade = jnp.exp2(old - new)
        acc[i, :, :T] *= fade
        acc[i, :, T:] *= fade

        def exps(n, _):
            c = base + n
            mm = mrun[i]
            s = s_ref[n]
            e = jnp.concatenate(
                [jnp.exp2(s[:, k * T:(k + 1) * T] - mm) for k in range(CH // T)], 1
            ).astype(BF)
            e_ref[off(i) + c] = e
            acc[i] += dot(e, va[chunk_rows(c), :], NN)
            return 0

        lax.fori_loop(0, count, exps, 0)

    def prefix_group(d, g):
        def tile(i, _):
            top = jnp.maximum(scores(i, 2 * d, 0), scores(i, 2 * d + 1, 1))
            weigh(i, 2 * d, 2, g, top)
            return 0

        lax.fori_loop(0, 4, tile, 0)

    def response_tile(i, _):
        top_ref[...] = jnp.full((R, T), -jnp.inf, F32)

        def one(n, _):
            top_ref[...] = jnp.maximum(top_ref[...], scores(i, PC + n, n))
            return 0

        lax.fori_loop(0, i, one, 0)
        s = dot(qa[i], ka[chunk_rows(PC + i), :], NT)
        col = lax.broadcasted_iota(jnp.int32, (T, CH), 1)
        row = lax.broadcasted_iota(jnp.int32, (T, CH), 0) + y * T
        seen = col <= row
        s = jnp.concatenate(
            [jnp.where(seen, s[h * T:(h + 1) * T], -jnp.inf) for h in range(HEADS)], 0
        )
        s_ref[i] = s
        weigh(i, PC, i + 1, 4, jnp.maximum(top_ref[...], fold(s)))
        stat[i] = jnp.exp2(stat[i] - mrun[i])
        pos = lax.broadcasted_iota(jnp.int32, (T, T), 0) + (i * CH + y * T)
        live = pos < lens_ref[resp]
        part = lax.broadcasted_iota(jnp.int32, (T, T), 1)
        for h in range(HEADS):
            rs = slice(h * T, (h + 1) * T)
            inv = 1.0 / acc[i, rs, T:]
            o = jnp.where(live, acc[i, rs, :T] * inv, 0.0).astype(BF)
            o_ref[i, :, rs] = o
            g = jnp.where(live, g_ref[i, :, rs].astype(F32), 0.0)
            d0 = -jnp.sum(g * o.astype(F32), 1, keepdims=True)
            d1 = d0.astype(BF).astype(F32)
            d2 = (d0 - d1).astype(BF).astype(F32)
            d3 = d0 - d1 - d2
            ga[i, rs, :T] = g.astype(BF)
            ga[i, rs, T:] = jnp.where(
                part == 0, d1, jnp.where(part == 1, d2, jnp.where(part == 2, d3, 0.0))
            ).astype(BF)
            gt[0, i, :, rs] = (q_ref[i, :, rs].astype(F32) * (inv * scale)).astype(BF).T
            gt[1, i, :, rs] = (g * inv).astype(BF).T
            turned[i, :, rs] = stat[i, rs, :].T[:8]
            acc[i, rs, T:] = inv * scale
        acc[i, :, :T] = jnp.zeros((R, T), F32)
        return 0

    order = (0, 2, 1, 3)
    place(0)
    prefix_group(0, 0)
    for g in (1, 2, 3):
        for copy in ygather[order[g]]:
            copy.wait()
        place(order[g])
        prefix_group(order[g], g)
    lax.fori_loop(0, 4, response_tile, 0)

    homes = []
    for d in range(4):
        tx = (x + d) % 4
        copy = local if d == 0 else functools.partial(remote, dev=xdev(d))
        homes.append(copy(o_ref.at[tx], attended.at[resp, :, wide(kvh)]))
    for copy in homes:
        copy.start()

    def scaled(g):
        def turn(i, _):
            f = turned[i, g:g + 1, :]
            for w in range(2):
                gs[w, i] = (gt[w, i].astype(F32) * f).astype(BF)
            return 0

        lax.fori_loop(0, 4, turn, 0)

    def grads(c, first, g):
        kk = chunk_rows(c)
        s_ref[0, :2 * T, :] = jnp.zeros((2 * T, CH), F32)

        def row(i, _):
            e = e_ref[off(i) + c]
            dp = dot(ga[i], va[kk, :], NT)
            ds = (e.astype(F32) * dp).astype(BF)
            acc[i, :, :T] += stat[i, :, g:g + 1] * dot(ds, ka[kk, :T], NN)
            s_ref[0, :T, :] += dot(gs[0, i], ds, NN)
            s_ref[0, T:2 * T, :] += dot(gs[1, i], e, NN)
            return 0

        lax.fori_loop(first, 4, row, 0)
        return [s_ref[0, w * T:(w + 1) * T, :].T.astype(BF) for w in range(2)]

    def response(i, _):
        for w, val in enumerate(grads(PC + i, i, 4)):
            for b in range(4):
                kv[b, w, pl.ds(mult(1024 + i * T, T), T), :] = val[b * T:(b + 1) * T]
        return 0

    scaled(4)
    lax.fori_loop(0, 4, response, 0)
    yback = []
    for d in (2, 1, 3):
        ty = (y + d) % 4
        copy = remote(kv.at[ty, :, pl.ds(1024, 512), :], rbuf.at[d - 1, :, pl.ds(1024, 512), :], ydev(d))
        copy.start()
        yback.append(copy)
    for d in (2, 1, 3, 0):
        ty = (y + d) % 4
        came = (4 - d) % 4
        scaled(order.index(came))

        def prefix(half, _):
            for w, val in enumerate(grads(came * 2 + half, 0, order.index(came))):
                kv[ty, w, pl.ds(mult(half * CH, CH), CH), :] = val
            return 0

        lax.fori_loop(0, 2, prefix, 0)
        if d:
            copy = remote(kv.at[ty, :, pl.ds(0, 1024), :], rbuf.at[d - 1, :, pl.ds(0, 1024), :], ydev(d))
            copy.start()
            yback.append(copy)

    for i in range(4):
        for h in range(HEADS):
            rs = slice(h * T, (h + 1) * T)
            dq_ref[i, :, rs] = (acc[i, rs, :T] * acc[i, rs, T:]).astype(BF)
    for d in range(4):
        tx = (x + d) % 4
        copy = local if d == 0 else functools.partial(remote, dev=xdev(d))
        homes.append(copy(dq_ref.at[tx], query_grad.at[resp, :, wide(kvh)]))
        homes[-1].start()

    for copy in yback:
        copy.wait()

    def total(b, _):
        for w in range(2):
            rs = pl.ds(mult(b * T, T), T)
            acc4 = kv[y, w, rs, :].astype(F32)
            for d in range(3):
                acc4 = acc4 + rbuf[d, w, rs, :].astype(F32)
            kv[y, w, rs, :] = acc4.astype(BF)
        return 0

    lax.fori_loop(0, 12, total, 0)
    tail = []
    for other in (1, 0):
        for d in range(4):
            tx, tg = (x + d) % 4, (grp + other) % 2
            copy = local if (d == 0 and not other) else functools.partial(remote, dev=xdev(d, other))
            tail.append(copy(kv.at[y, :, blk(tg * 4 + tx), :], pbuf.at[grp * 4 + x]))
    for d in range(4):
        tx = (x + d) % 4
        copy = local if d == 0 else functools.partial(remote, dev=xdev(d))
        for w, out in ((0, key_grad), (1, value_grad)):
            homes.append(copy(kv.at[y, w, blk(8 + tx), :], out.at[resp, :, hd(kvh)]))
            tail.append(homes.pop())
    for copy in tail:
        copy.start()
    for copy in tail[:8]:
        copy.wait()
    for j in range(2):
        for w, out in ((0, pk_grad), (1, pv_grad)):
            parts = [pbuf[gg * 4 + rr * 2 + j, w].astype(F32) for gg in range(2) for rr in range(2)]
            out[:, j * T:(j + 1) * T] = (parts[0] + parts[1] + parts[2] + parts[3]).astype(BF)
    for copy in tail[8:] + homes:
        copy.wait()
    assert counter[0] <= N_SEM and counter[1] <= N_SEM


def shards(queries, keys, values, prefix_keys, shared_prompt_values, lengths, grad_out):
    like = lambda a: jax.ShapeDtypeStruct(a.shape, BF)
    hbm = pl.BlockSpec(memory_space=pl.ANY)
    vmem = pl.BlockSpec(memory_space=pltpu.VMEM)
    V = pltpu.VMEM
    return pl.pallas_call(
        kernel,
        out_shape=[like(queries), like(queries), like(keys), like(keys), like(prefix_keys), like(prefix_keys)],
        in_specs=[pl.BlockSpec(memory_space=pltpu.SMEM)] + [hbm] * 6,
        out_specs=[hbm] * 4 + [vmem] * 2,
        scratch_shapes=[
            V((4, T, R), BF), V((4, T, R), BF), V((4, 2, 1536, T), BF), V((3, 2, 1536, T), BF),
            V((8, 2, T, T), BF), V((4, T, R), BF), V((4, T, R), BF),
            V((6144, 256), BF), V((6144, 256), BF), V((4, R, 256), BF), V((4, R, 256), BF),
            V((2, 4, T, R), BF), V((2, 4, T, R), BF), V((4, R, CH), F32), V((42, R, CH), BF),
            V((4, R, T), F32), V((4, R, T), F32), V((4, 8, R), F32), V((R, T), F32), V((4, R, 256), F32),
            pltpu.SemaphoreType.DMA((N_SEM,)), pltpu.SemaphoreType.DMA((N_SEM,)),
            pltpu.SemaphoreType.DMA((N_SEM,)),
        ],
        compiler_params=pltpu.CompilerParams(
            collective_id=0, has_side_effects=True, vmem_limit_bytes=64 * 1024 * 1024
        ),
        name="attention",
    )(lengths, queries, keys, values, prefix_keys, shared_prompt_values, grad_out)


def solution(mesh):
    acts, prompt = P("grp", "ctx", "head"), P(("grp", "ctx"), "head")
    return jax.shard_map(
        shards,
        mesh=mesh,
        in_specs=(acts, acts, acts, prompt, prompt, P("grp"), acts),
        out_specs=(acts, acts, acts, acts, prompt, prompt),
        check_vma=False,
    )
```

time: 1140 us -> 143 us (0.13)
  waiting for transfers between devices: 725 us -> 0 us
  matrix products: 267 us -> 0 us
  Pallas kernels: 0 us -> 136 us
  local copies, waits for them, and re-layouts: 90.5 us -> 6.36 us
  other arithmetic: 39.9 us -> 0 us
  between operations: 14.3 us -> 0.66 us
    reduce_scatter x4 -> x0, waiting for transfers between devices: 508 us -> none  [the longest x1 188 us: shards(): lax.psum_scatter(pv_part, ('grp', 'ctx'), scatter_dimension=0, tiled=True)]
    dot_general x30 -> x0, matrix products: 267 us -> none  [the longest x5 76.3 us: step(): jnp.einsum('rktu,rtkd->rukd', plow, ggroup, preferred_element_type=jnp.fl...]
    all_gather x4 -> x0, waiting for transfers between devices: 215 us -> none  [the longest x1 70.8 us: shards(): lax.all_gather(prefix_keys, ('grp', 'ctx'), axis=0, tiled=True)]
    pallas_call x0 -> x1, Pallas kernels: none -> 136 us  [shards(): pl.pallas_call(kernel, out_shape=[like(queries), like(queries), like(keys...]
    while x40 -> x0, local copies, waits for them, and re-layouts: 26.8 us -> none
    reduce_sum x6 -> x0, other arithmetic: 20 us -> none  [the longest x1 10.4 us: shards(): pv_part = jnp.sum(value_gradient[:, :pcount], 0).reshape(pcount, kwidth)]
    all_gather x3 -> x0, local copies, waits for them, and re-layouts: 12.2 us -> none  [the longest x1 4.14 us: shards(): lax.all_gather(shared_prompt_values, ('grp', 'ctx'), axis=0, tiled=True)]
  transfers between devices with their start and end apart: 8 -> 0, of which waited for: 8 -> 0; matrix products, arithmetic and copies ran while one was open for 4% -> 0% of each run, Pallas kernels for 0% -> 0%
where the time goes in v1:
time: 143 us
  Pallas kernels  136 us (95%)
  local copies, waits for them, and re-layouts  6.36 us (4%)
    pallas_call x1, Pallas kernels, shards(): pl.pallas_call(kernel, out_shape=[like(queries), like(queries), like(keys...  136 us
    unnamed x16, local copies, waits for them, and re-layouts  6.36 us

profile of v1, /device:TPU:0, one launch (start us, length us, event | category | flops | bytes accessed | tf_op | source)
XLA Modules:
  0.0 142.6 jit_solution(10214688308113725048)
XLA Ops:
  0.6 135.6 %attention.1 = (bf16[2,128,1280]{2,1,0:T(8,128)(2,1)}, bf16[2,128,1280]{2,1,0:T(8,128)(2,1)}, bf16[2,128,256]{2,1,0:T(8,128)(2,1)}, bf16[2,128,256]{2,1,0:T(8,12...) custom-call(s32[2]{0:T(128)} %lens_ref.1, bf16[2,128,1280]{2,1,0:T(8,128)(2,1)} %queries.1, ...), custom_call_target="tpu_custom_call" | custom-call | tf_op jit(solution)/shard_map/attention/pallas_call | solution.py:352
  136.3 0.0 copy-start
  136.3 2.0 %copy.19 = bf16[2,128,1280]{2,1,0:T(8,128)(2,1)} copy(bf16[2,128,1280]{2,1,0:T(8,128)(2,1)} %get-tuple-element.12) | data formatting | bytes 1310720
  138.3 0.0 copy-done
  138.3 0.0 copy-start.2
  138.3 0.8 copy.20
  139.1 0.2 copy-done.2
  139.3 0.0 copy-start.1
  139.3 0.7 copy.21
  140.0 0.3 copy-done.1
  140.3 0.0 copy-start.4
  140.3 0.7 copy.22
  140.9 0.2 copy-done.4
  141.1 0.0 copy-start.3
  141.1 0.6 copy.23
  141.8 0.2 copy-done.3
  142.0 0.6 copy.24
Async XLA Ops:
  136.3 2.0 %copy-start = (bf16[2,128,1280]{2,1,0:T(8,128)(2,1)S(1)}, bf16[2,128,1280]{2,1,0:T(8,128)(2,1)}, u32[]{:S(2)}) copy-start(bf16[2,128,1280]{2,1,0:T(8,128)(2,1)} %get-tuple-element.13) | copy-start | bytes 1966084
  138.3 1.0 copy-start.2
  139.3 1.0 copy-start.1
  140.3 0.9 copy-start.4
  141.1 0.9 copy-start.3

commit v2 on v1

v2 whole, which is shorter than its diff:
```python
import functools
import math

import jax
import jax.numpy as jnp
from jax import lax
from jax.experimental import pallas as pl
from jax.experimental.pallas import tpu as pltpu
from jax.sharding import PartitionSpec as P

MESH = pl.DeviceIdType.MESH
F32, BF = jnp.float32, jnp.bfloat16
T = 128
CH = 512
HEADS = 5
R = HEADS * T
PC = 8
NT = (((1,), (1,)), ((), ()))
NN = (((1,), (0,)), ((), ()))
dot = functools.partial(lax.dot_general, preferred_element_type=F32)
N_SEM = 64


def mult(v, n):
    return pl.multiple_of(v, n)


def kernel(
    lens_ref, queries, keys, values, pkeys, pvalues, gout,
    attended, query_grad, key_grad, value_grad, pk_grad, pv_grad,
    q_ref, g_ref, kv, rbuf, pbuf,
    ka, va, qa, gt, gs, s_ref, ds_ref, e_ref, mrun, stat, turned, top_ref, acc,
    send, recv, lsem,
):
    grp, ctx, head = lax.axis_index("grp"), lax.axis_index("ctx"), lax.axis_index("head")
    x, y = ctx // 4, ctx % 4
    resp, kvh = x // 2, x % 2
    c2 = 1.4426950408889634 / math.sqrt(T)
    scale = 1.0 / math.sqrt(T)

    def xdev(d, other=0):
        return ((grp + other) % 2, ((x + d) % 4) * 4 + y, head)

    def ydev(d):
        return (grp, x * 4 + (y + d) % 4, head)

    counter = [0, 0]

    def remote(src, dst, dev):
        k = counter[0]
        counter[0] += 1
        return pltpu.make_async_remote_copy(
            src_ref=src, dst_ref=dst, send_sem=send.at[k], recv_sem=recv.at[k],
            device_id=dev, device_id_type=MESH,
        )

    def local(src, dst):
        k = counter[1]
        counter[1] += 1
        return pltpu.make_async_copy(src, dst, lsem.at[k])

    partners = [xdev(d) for d in (1, 2, 3)] + [ydev(d) for d in (1, 2, 3)] + [xdev(d, 1) for d in range(4)]
    barrier = pltpu.get_barrier_semaphore()
    for dev in partners:
        pl.semaphore_signal(barrier, inc=1, device_id=dev, device_id_type=MESH)
    pl.semaphore_wait(barrier, len(partners))

    def hd(j):
        return pl.ds(mult(j * T, T), T)

    def wide(j):
        return pl.ds(mult(j * R, T), R)

    def blk(b):
        return pl.ds(mult(b * T, T), T)

    pre, own, late = [], [], []
    for other in (0, 1):
        for d in range(4):
            tx = (x + d) % 4
            j = tx % 2
            here = d == 0 and not other
            copy = local if here else functools.partial(remote, dev=xdev(d, other))
            for which, ref in ((0, pkeys), (1, pvalues)):
                pre.append(copy(ref.at[:, hd(j)], kv.at[y, which, blk(grp * 4 + x), :]))
    for d in range(4):
        tx = (x + d) % 4
        r, j = tx // 2, tx % 2
        copy = local if d == 0 else functools.partial(remote, dev=xdev(d))
        for which, ref in ((0, keys), (1, values)):
            pre.append(copy(ref.at[r, :, hd(j)], kv.at[y, which, blk(8 + x), :]))
        for ref, buf in ((queries, q_ref), (gout, g_ref)):
            (late if d else own).append(copy(ref.at[r, :, wide(j)], buf.at[x]))
    for copy in pre + own:
        copy.start()
    for copy in own + pre:
        copy.wait()
    asked, graded = late[0::2], late[1::2]
    for copy in asked:
        copy.start()

    front, back = pl.ds(0, 1024), pl.ds(1024, 512)

    def near(rows):
        return [remote(kv.at[y, :, rows, :], kv.at[y, :, rows, :], ydev(d)) for d in (1, 3)]

    def far(rows):
        up, down = (y + 1) % 4, (y + 3) % 4
        return [
            remote(kv.at[up, 0, rows, :], kv.at[up, 0, rows, :], ydev(3)),
            remote(kv.at[down, 1, rows, :], kv.at[down, 1, rows, :], ydev(1)),
        ]

    near_front, near_back, far_front, far_back = near(front), near(back), far(front), far(back)
    for copy in near_front:
        copy.start()

    def place(d):
        sy = (y - d) % 4
        ps = pl.ds(d * 1024, 1024)
        ka[ps, :T] = kv[sy, 0, :1024, :]
        ka[ps, T:] = kv[sy, 0, :1024, :]
        va[ps, :T] = kv[sy, 1, :1024, :]
        va[ps, T:] = jnp.ones((1024, T), BF)

    def place_response():
        for sy in range(4):
            for i in range(4):
                rs = slice(4096 + i * CH + sy * T, 4096 + i * CH + (sy + 1) * T)
                src = slice(1024 + i * T, 1024 + (i + 1) * T)
                ka[rs, :T] = kv[sy, 0, src, :]
                ka[rs, T:] = kv[sy, 0, src, :]
                va[rs, :T] = kv[sy, 1, src, :]
                va[rs, T:] = jnp.ones((T, T), BF)

    def slot(c, i):
        n = c - PC
        return jnp.where(n < 0, 4 * c + i, 32 + 4 * n - (n * (n - 1)) // 2 + i - n)

    def chunk_rows(c):
        return pl.ds(mult(c * CH, CH), CH)

    def fold(s):
        return functools.reduce(jnp.maximum, [s[:, k * T:(k + 1) * T] for k in range(CH // T)])

    lane = lax.broadcasted_iota(jnp.int32, (R, T), 1)

    def prepare(i, _):
        for h in range(HEADS):
            rs = slice(h * T, (h + 1) * T)
            qs = q_ref[i, :, rs].astype(F32) * c2
            hi = qs.astype(BF)
            qa[i, rs, :T] = hi
            qa[i, rs, T:] = (qs - hi.astype(F32)).astype(BF)
        acc[i] = jnp.zeros((R, 2 * T), F32)
        mrun[i] = jnp.full((R, T), -jnp.inf, F32)
        stat[i] = jnp.zeros((R, T), F32)
        return 0

    def scores(i, c, slot):
        s = dot(qa[i], ka[chunk_rows(c), :], NT)
        s_ref[slot] = s
        return fold(s)

    def weigh(i, base, count, g, top):
        old = mrun[i]
        new = jnp.maximum(old, jnp.broadcast_to(jnp.max(top, 1, keepdims=True), (R, T)))
        mrun[i] = new
        stat[i] = jnp.where(lane == g, new, stat[i])
        fade = jnp.exp2(old - new)
        acc[i, :, :T] *= fade
        acc[i, :, T:] *= fade

        def exps(n, _):
            c = base + n
            mm = mrun[i]
            s = s_ref[n]
            e = jnp.concatenate(
                [jnp.exp2(s[:, k * T:(k + 1) * T] - mm) for k in range(CH // T)], 1
            ).astype(BF)
            e_ref[slot(c, i)] = e
            acc[i] += dot(e, va[chunk_rows(c), :], NN)
            return 0

        lax.fori_loop(0, count, exps, 0)

    def prefix_tile(i, d, g):
        top = jnp.maximum(scores(i, 2 * d, 0), scores(i, 2 * d + 1, 1))
        weigh(i, 2 * d, 2, g, top)

    def prefix_group(d, g, first):
        def tile(n, _):
            prefix_tile((x + n) % 4, d, g)
            return 0

        lax.fori_loop(first, 4, tile, 0)

    def response_tile(i, _):
        top_ref[...] = jnp.full((R, T), -jnp.inf, F32)

        def one(n, _):
            top_ref[...] = jnp.maximum(top_ref[...], scores(i, PC + n, n))
            return 0

        lax.fori_loop(0, i, one, 0)
        s = dot(qa[i], ka[chunk_rows(PC + i), :], NT)
        col = lax.broadcasted_iota(jnp.int32, (T, CH), 1)
        row = lax.broadcasted_iota(jnp.int32, (T, CH), 0) + y * T
        seen = col <= row
        s = jnp.concatenate(
            [jnp.where(seen, s[h * T:(h + 1) * T], -jnp.inf) for h in range(HEADS)], 0
        )
        s_ref[i] = s
        weigh(i, PC, i + 1, 4, jnp.maximum(top_ref[...], fold(s)))
        stat[i] = jnp.exp2(stat[i] - mrun[i])
        pos = lax.broadcasted_iota(jnp.int32, (T, T), 0) + (i * CH + y * T)
        live = pos < lens_ref[resp]
        part = lax.broadcasted_iota(jnp.int32, (T, T), 1)
        for h in range(HEADS):
            rs = slice(h * T, (h + 1) * T)
            inv = 1.0 / acc[i, rs, T:]
            o = jnp.where(live, acc[i, rs, :T] * inv, 0.0).astype(BF)
            g = jnp.where(live, g_ref[i, :, rs].astype(F32), 0.0)
            g_ref[i, :, rs] = o
            d0 = -jnp.sum(g * o.astype(F32), 1, keepdims=True)
            d1 = d0.astype(BF).astype(F32)
            d2 = (d0 - d1).astype(BF).astype(F32)
            d3 = d0 - d1 - d2
            qa[i, rs, :T] = g.astype(BF)
            qa[i, rs, T:] = jnp.where(
                part == 0, d1, jnp.where(part == 1, d2, jnp.where(part == 2, d3, 0.0))
            ).astype(BF)
            gt[0, i, :, rs] = (q_ref[i, :, rs].astype(F32) * (inv * scale)).astype(BF).T
            gt[1, i, :, rs] = (g * inv).astype(BF).T
            turned[i, :, rs] = stat[i, rs, :].T[:8]
            acc[i, rs, T:] = inv * scale
        acc[i, :, :T] = jnp.zeros((R, T), F32)
        return 0

    order = (0, 1, 3, 2)
    place(0)
    prepare(x, 0)
    prefix_tile(x, 0, 0)
    for copy in asked:
        copy.wait()
    for copy in graded:
        copy.start()
    lax.fori_loop(1, 4, lambda n, _: prepare((x + n) % 4, 0), 0)
    prefix_group(0, 0, 1)
    for copy in near_front:
        copy.wait()
    for copy in far_front + near_back:
        copy.start()
    for g in (1, 2):
        place(order[g])
        prefix_group(order[g], g, 0)
    for copy in near_back:
        copy.wait()
    for copy in far_back:
        copy.start()
    for copy in far_front:
        copy.wait()
    place(2)
    prefix_group(2, 3, 0)
    for copy in far_back + graded:
        copy.wait()
    place_response()
    lax.fori_loop(0, 4, response_tile, 0)

    homes = []
    for d in range(4):
        tx = (x + d) % 4
        copy = local if d == 0 else functools.partial(remote, dev=xdev(d))
        homes.append(copy(g_ref.at[tx], attended.at[resp, :, wide(kvh)]))
    for copy in homes:
        copy.start()

    def scaled(g):
        for i in range(4):
            f = turned[i, g:g + 1, :]
            for w in range(2):
                gs[w, :, i * R:(i + 1) * R] = (gt[w, i].astype(F32) * f).astype(BF)

    def rows_part(i, c, g, buf):
        kk = chunk_rows(c)
        dp = dot(qa[i], va[kk, :], NT)
        ds = (e_ref[slot(c, i)].astype(F32) * dp).astype(BF)
        ds_ref[buf, i] = ds
        acc[i, :, :T] += stat[i, :, g:g + 1] * dot(ds, ka[kk, :T], NN)

    def keys_part(c, first, buf):
        n = (4 - first) * R
        base = slot(c, first)
        ds = ds_ref[buf, first:].reshape(n, CH)
        e = e_ref[pl.ds(base, 4 - first)].reshape(n, CH)
        dk = dot(gs[0, :, first * R:], ds, NN)
        dv = dot(gs[1, :, first * R:], e, NN)
        return dk.T.astype(BF), dv.T.astype(BF)

    def all_rows(c, first, g, buf):
        lax.fori_loop(first, 4, lambda i, _: (rows_part(i, c, g, buf), 0)[1], 0)

    scaled(4)
    for i in range(4):
        all_rows(PC + i, i, 4, 0)
        for w, val in enumerate(keys_part(PC + i, i, 0)):
            for b in range(4):
                kv[b, w, 1024 + i * T:1024 + (i + 1) * T, :] = val[b * T:(b + 1) * T]
    yback_resp, yback = [], []
    for d in (2, 1, 3):
        ty = (y + d) % 4
        yback_resp.append(remote(kv.at[ty, :, back, :], rbuf.at[d - 1, :, back, :], ydev(d)))
        yback_resp[-1].start()

    def total(b, _):
        for w in range(2):
            rs = pl.ds(mult(b * T, T), T)
            acc4 = kv[y, w, rs, :].astype(F32)
            for d in range(3):
                acc4 = acc4 + rbuf[d, w, rs, :].astype(F32)
            kv[y, w, rs, :] = acc4.astype(BF)
        return 0

    for d in (2, 1, 3, 0):
        ty = (y + d) % 4
        came = (4 - d) % 4
        g = order.index(came)
        scaled(g)

        def finish(half, _):
            for w, val in enumerate(keys_part(came * 2 + half, 0, half)):
                kv[ty, w, pl.ds(mult(half * CH, CH), CH), :] = val
            return 0

        def both(half, _):
            all_rows(came * 2 + half, 0, g, half)
            return 0

        lax.fori_loop(0, 2, both, 0)
        if d == 0:
            for i in range(4):
                for h in range(HEADS):
                    rs = slice(h * T, (h + 1) * T)
                    q_ref[i, :, rs] = (acc[i, rs, :T] * acc[i, rs, T:]).astype(BF)
            for e in (2, 1, 3, 0):
                tx = (x + e) % 4
                copy = local if e == 0 else functools.partial(remote, dev=xdev(e))
                homes.append(copy(q_ref.at[tx], query_grad.at[resp, :, wide(kvh)]))
                homes[-1].start()
        lax.fori_loop(0, 2, finish, 0)
        if d:
            yback.append(remote(kv.at[ty, :, front, :], rbuf.at[d - 1, :, front, :], ydev(d)))
            yback[-1].start()
        if d == 3:
            for copy in yback_resp:
                copy.wait()
            lax.fori_loop(8, 12, total, 0)
            for e in range(4):
                tx = (x + e) % 4
                copy = local if e == 0 else functools.partial(remote, dev=xdev(e))
                for w, out in ((0, key_grad), (1, value_grad)):
                    homes.append(copy(kv.at[y, w, blk(8 + tx), :], out.at[resp, :, hd(kvh)]))
                    homes[-1].start()

    for copy in yback:
        copy.wait()
    lax.fori_loop(0, 8, total, 0)
    tail = []
    for other in (1, 0):
        for d in (2, 1, 3, 0):
            tx, tg = (x + d) % 4, (grp + other) % 2
            copy = local if (d == 0 and not other) else functools.partial(remote, dev=xdev(d, other))
            tail.append(copy(kv.at[y, :, blk(tg * 4 + tx), :], pbuf.at[grp * 4 + x]))
            tail[-1].start()
    for copy in tail:
        copy.wait()
    for j in range(2):
        for w, out in ((0, pk_grad), (1, pv_grad)):
            parts = [pbuf[gg * 4 + rr * 2 + j, w].astype(F32) for gg in range(2) for rr in range(2)]
            out[:, j * T:(j + 1) * T] = (parts[0] + parts[1] + parts[2] + parts[3]).astype(BF)
    for copy in homes:
        copy.wait()
    assert counter[0] <= N_SEM and counter[1] <= N_SEM


def settle(*refs):
    n = len(refs) // 3
    arrived, left = refs[3 * n:]
    loads = [pltpu.make_async_copy(refs[k], refs[2 * n + k], arrived.at[k]) for k in range(n)]
    stores = [pltpu.make_async_copy(refs[2 * n + k], refs[n + k], left.at[k]) for k in range(n)]
    for copy in loads:
        copy.start()
    for load, store in zip(loads, stores):
        load.wait()
        store.start()
    for copy in stores:
        copy.wait()


def shards(queries, keys, values, prefix_keys, shared_prompt_values, lengths, grad_out):
    like = lambda a: jax.ShapeDtypeStruct(a.shape, BF)
    hbm = pl.BlockSpec(memory_space=pl.ANY)
    vmem = pl.BlockSpec(memory_space=pltpu.VMEM)
    V = pltpu.VMEM
    shapes = [like(queries), like(queries), like(keys), like(keys), like(prefix_keys), like(prefix_keys)]
    made = pl.pallas_call(
        kernel,
        out_shape=shapes,
        in_specs=[pl.BlockSpec(memory_space=pltpu.SMEM)] + [hbm] * 6,
        out_specs=[hbm] * 4 + [vmem] * 2,
        scratch_shapes=[
            V((4, T, R), BF), V((4, T, R), BF), V((4, 2, 1536, T), BF), V((3, 2, 1536, T), BF),
            V((8, 2, T, T), BF),
            V((6144, 256), BF), V((6144, 256), BF), V((4, R, 256), BF),
            V((2, 4, T, R), BF), V((2, T, 4 * R), BF), V((4, R, CH), F32), V((2, 4, R, CH), BF), V((42, R, CH), BF),
            V((4, R, T), F32), V((4, R, T), F32), V((4, 8, R), F32), V((R, T), F32), V((4, R, 256), F32),
            pltpu.SemaphoreType.DMA((N_SEM,)), pltpu.SemaphoreType.DMA((N_SEM,)),
            pltpu.SemaphoreType.DMA((N_SEM,)),
        ],
        compiler_params=pltpu.CompilerParams(
            collective_id=0, has_side_effects=True, vmem_limit_bytes=64 * 1024 * 1024
        ),
        name="attention",
    )(lengths, queries, keys, values, prefix_keys, shared_prompt_values, grad_out)
    return pl.pallas_call(
        settle,
        out_shape=shapes,
        in_specs=[hbm] * 6,
        out_specs=[hbm] * 6,
        scratch_shapes=[V(a.shape, BF) for a in shapes] + [pltpu.SemaphoreType.DMA((6,))] * 2,
        name="settle",
    )(*made)


def solution(mesh):
    acts, prompt = P("grp", "ctx", "head"), P(("grp", "ctx"), "head")
    return jax.shard_map(
        shards,
        mesh=mesh,
        in_specs=(acts, acts, acts, prompt, prompt, P("grp"), acts),
        out_specs=(acts, acts, acts, acts, prompt, prompt),
        check_vma=False,
    )
```

time: 143 us -> 118 us (0.83)
  Pallas kernels: 136 us -> 117 us
  local copies, waits for them, and re-layouts: 6.36 us -> 0 us
    pallas_call x1 -> x2, Pallas kernels: 136 us -> 117 us  [the longest x1 115 us: shards(): pl.pallas_call(kernel, out_shape=shapes, in_specs=[pl.BlockSpec(memory_sp...]
    unnamed x16 -> x0, local copies, waits for them, and re-layouts: 6.36 us -> none
where the time goes in v2:
time: 118 us
  Pallas kernels  117 us (99%)
    pallas_call x1, Pallas kernels, shards(): pl.pallas_call(kernel, out_shape=shapes, in_specs=[pl.BlockSpec(memory_sp...  115 us
    pallas_call x1, Pallas kernels, shards(): pl.pallas_call(settle, out_shape=shapes, in_specs=[hbm] * 6, out_specs=[h...  2.36 us

profile of v2, /device:TPU:0, one launch (start us, length us, event | category | flops | bytes accessed | tf_op | source)
XLA Modules:
  0.0 117.9 jit_solution(7332421930145354159)
XLA Ops:
  0.6 114.8 %attention.1 = (bf16[2,128,1280]{2,1,0:T(8,128)(2,1)}, bf16[2,128,1280]{2,1,0:T(8,128)(2,1)}, bf16[2,128,256]{2,1,0:T(8,128)(2,1)}, bf16[2,128,256]{2,1,0:T(8,12...) custom-call(s32[2]{0:T(128)} %lens_ref.1, bf16[2,128,1280]{2,1,0:T(8,128)(2,1)} %queries.1, ...), custom_call_target="tpu_custom_call" | custom-call | tf_op jit(solution)/shard_map/attention/pallas_call | solution.py:406
  115.4 2.4 %settle.1 = (bf16[2,128,1280]{2,1,0:T(8,128)(2,1)}, bf16[2,128,1280]{2,1,0:T(8,128)(2,1)}, bf16[2,128,256]{2,1,0:T(8,128)(2,1)}, bf16[2,128,256]{2,1,0:T(8,128)(...) custom-call(bf16[2,128,1280]{2,1,0:T(8,128)(2,1)} %get-tuple-element.12.refs_0_, ...), custom_call_target="tpu_custom_call" | custom-call | tf_op jit(solution)/shard_map/settle/pallas_call | solution.py:425

commit v3 on v2

--- a/solution.py
+++ b/solution.py
@@ -71,66 +71,79 @@
     def wide(j):
         return pl.ds(mult(j * R, T), R)
 
-    def blk(b):
-        return pl.ds(mult(b * T, T), T)
-
     pre, own, late = [], [], []
-    for other in (0, 1):
-        for d in range(4):
-            tx = (x + d) % 4
-            j = tx % 2
-            here = d == 0 and not other
-            copy = local if here else functools.partial(remote, dev=xdev(d, other))
-            for which, ref in ((0, pkeys), (1, pvalues)):
-                pre.append(copy(ref.at[:, hd(j)], kv.at[y, which, blk(grp * 4 + x), :]))
+    for d in range(4):
+        j = (x + d) % 2
+        copy = local if d == 0 else functools.partial(remote, dev=xdev(d))
+        for which, ref in ((0, pkeys), (1, pvalues)):
+            pre.append(copy(ref.at[:, hd(j)], kv.at[y, grp, x, which]))
     for d in range(4):
         tx = (x + d) % 4
         r, j = tx // 2, tx % 2
         copy = local if d == 0 else functools.partial(remote, dev=xdev(d))
         for which, ref in ((0, keys), (1, values)):
-            pre.append(copy(ref.at[r, :, hd(j)], kv.at[y, which, blk(8 + x), :]))
+            pre.append(copy(ref.at[r, :, hd(j)], kv.at[y, 2, x, which]))
         for ref, buf in ((queries, q_ref), (gout, g_ref)):
             (late if d else own).append(copy(ref.at[r, :, wide(j)], buf.at[x]))
     for copy in pre + own:
         copy.start()
-    for copy in own + pre:
-        copy.wait()
     asked, graded = late[0::2], late[1::2]
-    for copy in asked:
-        copy.start()
-
-    front, back = pl.ds(0, 1024), pl.ds(1024, 512)
-
-    def near(rows):
-        return [remote(kv.at[y, :, rows, :], kv.at[y, :, rows, :], ydev(d)) for d in (1, 3)]
-
-    def far(rows):
-        up, down = (y + 1) % 4, (y + 3) % 4
+
+    up, down = (y + 1) % 4, (y + 3) % 4
+
+    def near(part):
+        return [remote(kv.at[y, part], kv.at[y, part], ydev(d)) for d in (1, 3)]
+
+    def far(part):
+        low, high = pl.ds(0, 2), pl.ds(2, 2)
         return [
-            remote(kv.at[up, 0, rows, :], kv.at[up, 0, rows, :], ydev(3)),
-            remote(kv.at[down, 1, rows, :], kv.at[down, 1, rows, :], ydev(1)),
+            remote(kv.at[up, part, low], kv.at[up, part, low], ydev(3)),
+            remote(kv.at[down, part, high], kv.at[down, part, high], ydev(1)),
         ]
 
-    near_front, near_back, far_front, far_back = near(front), near(back), far(front), far(back)
-    for copy in near_front:
-        copy.start()
-
-    def place(d):
+    def across(d):
         sy = (y - d) % 4
-        ps = pl.ds(d * 1024, 1024)
-        ka[ps, :T] = kv[sy, 0, :1024, :]
-        ka[ps, T:] = kv[sy, 0, :1024, :]
-        va[ps, :T] = kv[sy, 1, :1024, :]
-        va[ps, T:] = jnp.ones((1024, T), BF)
+        return [remote(kv.at[sy, grp], kv.at[sy, grp], xdev(0, 1))]
+
+    near_prompt, near_resp, far_prompt, far_resp = near(grp), near(2), far(grp), far(2)
+    swap = {d: across(d) for d in range(4)}
+
+    def start(copies):
+        for copy in copies:
+            copy.start()
+
+    def wait(copies):
+        for copy in copies:
+            copy.wait()
+
+    wait(pre[:8])
+    start(near_prompt + swap[0])
+    wait(pre[8:])
+    start(asked)
+
+    OWN, OTHER = 0, 1
+    uses = [(0, OWN), (0, OTHER), (1, OWN), (3, OWN), (1, OTHER), (2, OWN), (3, OTHER), (2, OTHER)]
+
+    def half(kind):
+        return (grp + kind) % 2
+
+    def place(p):
+        d, kind = uses[p]
+        sy = (y - d) % 4
+        for b in range(4):
+            rs = slice(p * CH + b * T, p * CH + (b + 1) * T)
+            ka[rs, :T] = kv[sy, half(kind), b, 0]
+            ka[rs, T:] = kv[sy, half(kind), b, 0]
+            va[rs, :T] = kv[sy, half(kind), b, 1]
+            va[rs, T:] = jnp.ones((T, T), BF)
 
     def place_response():
         for sy in range(4):
             for i in range(4):
                 rs = slice(4096 + i * CH + sy * T, 4096 + i * CH + (sy + 1) * T)
-                src = slice(1024 + i * T, 1024 + (i + 1) * T)
-                ka[rs, :T] = kv[sy, 0, src, :]
-                ka[rs, T:] = kv[sy, 0, src, :]
-                va[rs, :T] = kv[sy, 1, src, :]
+                ka[rs, :T] = kv[sy, 2, i, 0]
+                ka[rs, T:] = kv[sy, 2, i, 0]
+                va[rs, :T] = kv[sy, 2, i, 1]
                 va[rs, T:] = jnp.ones((T, T), BF)
 
     def slot(c, i):
@@ -184,16 +197,16 @@
 
         lax.fori_loop(0, count, exps, 0)
 
-    def prefix_tile(i, d, g):
-        top = jnp.maximum(scores(i, 2 * d, 0), scores(i, 2 * d + 1, 1))
-        weigh(i, 2 * d, 2, g, top)
-
-    def prefix_group(d, g, first):
-        def tile(n, _):
-            prefix_tile((x + n) % 4, d, g)
+    def prefix_group(g):
+        place(2 * g)
+        place(2 * g + 1)
+
+        def tile(i, _):
+            top = jnp.maximum(scores(i, 2 * g, 0), scores(i, 2 * g + 1, 1))
+            weigh(i, 2 * g, 2, g, top)
             return 0
 
-        lax.fori_loop(first, 4, tile, 0)
+        lax.fori_loop(0, 4, tile, 0)
 
     def response_tile(i, _):
         top_ref[...] = jnp.full((R, T), -jnp.inf, F32)
@@ -237,33 +250,23 @@
         acc[i, :, :T] = jnp.zeros((R, T), F32)
         return 0
 
-    order = (0, 1, 3, 2)
-    place(0)
-    prepare(x, 0)
-    prefix_tile(x, 0, 0)
-    for copy in asked:
-        copy.wait()
-    for copy in graded:
-        copy.start()
-    lax.fori_loop(1, 4, lambda n, _: prepare((x + n) % 4, 0), 0)
-    prefix_group(0, 0, 1)
-    for copy in near_front:
-        copy.wait()
-    for copy in far_front + near_back:
-        copy.start()
-    for g in (1, 2):
-        place(order[g])
-        prefix_group(order[g], g, 0)
-    for copy in near_back:
-        copy.wait()
-    for copy in far_back:
-        copy.start()
-    for copy in far_front:
-        copy.wait()
-    place(2)
-    prefix_group(2, 3, 0)
-    for copy in far_back + graded:
-        copy.wait()
+    wait(own + asked)
+    start(graded)
+    lax.fori_loop(0, 4, prepare, 0)
+    wait(near_prompt + swap[0])
+    start(swap[1] + far_prompt + near_resp)
+    prefix_group(0)
+    wait(swap[1])
+    start(swap[3])
+    prefix_group(1)
+    wait(far_prompt)
+    start(swap[2])
+    wait(near_resp)
+    start(far_resp)
+    prefix_group(2)
+    wait(swap[3] + swap[2])
+    prefix_group(3)
+    wait(far_resp + graded)
     place_response()
     lax.fori_loop(0, 4, response_tile, 0)
 
@@ -281,105 +284,100 @@
             for w in range(2):
                 gs[w, :, i * R:(i + 1) * R] = (gt[w, i].astype(F32) * f).astype(BF)
 
-    def rows_part(i, c, g, buf):
+    def rows_part(i, c, g):
         kk = chunk_rows(c)
         dp = dot(qa[i], va[kk, :], NT)
         ds = (e_ref[slot(c, i)].astype(F32) * dp).astype(BF)
-        ds_ref[buf, i] = ds
+        ds_ref[i] = ds
         acc[i, :, :T] += stat[i, :, g:g + 1] * dot(ds, ka[kk, :T], NN)
 
-    def keys_part(c, first, buf):
+    def keys_part(c, first):
         n = (4 - first) * R
         base = slot(c, first)
-        ds = ds_ref[buf, first:].reshape(n, CH)
+        ds = ds_ref[first:].reshape(n, CH)
         e = e_ref[pl.ds(base, 4 - first)].reshape(n, CH)
         dk = dot(gs[0, :, first * R:], ds, NN)
         dv = dot(gs[1, :, first * R:], e, NN)
         return dk.T.astype(BF), dv.T.astype(BF)
 
-    def all_rows(c, first, g, buf):
-        lax.fori_loop(first, 4, lambda i, _: (rows_part(i, c, g, buf), 0)[1], 0)
+    def all_rows(c, first, g):
+        lax.fori_loop(first, 4, lambda i, _: (rows_part(i, c, g), 0)[1], 0)
 
     scaled(4)
     for i in range(4):
-        all_rows(PC + i, i, 4, 0)
-        for w, val in enumerate(keys_part(PC + i, i, 0)):
+        all_rows(PC + i, i, 4)
+        for w, val in enumerate(keys_part(PC + i, i)):
             for b in range(4):
-                kv[b, w, 1024 + i * T:1024 + (i + 1) * T, :] = val[b * T:(b + 1) * T]
-    yback_resp, yback = [], []
-    for d in (2, 1, 3):
+                kv[b, 2, i, w] = val[b * T:(b + 1) * T]
+
+    def send_back(d, part):
         ty = (y + d) % 4
-        yback_resp.append(remote(kv.at[ty, :, back, :], rbuf.at[d - 1, :, back, :], ydev(d)))
-        yback_resp[-1].start()
-
-    def total(b, _):
-        for w in range(2):
-            rs = pl.ds(mult(b * T, T), T)
-            acc4 = kv[y, w, rs, :].astype(F32)
-            for d in range(3):
-                acc4 = acc4 + rbuf[d, w, rs, :].astype(F32)
-            kv[y, w, rs, :] = acc4.astype(BF)
-        return 0
-
-    for d in (2, 1, 3, 0):
-        ty = (y + d) % 4
-        came = (4 - d) % 4
-        g = order.index(came)
-        scaled(g)
-
-        def finish(half, _):
-            for w, val in enumerate(keys_part(came * 2 + half, 0, half)):
-                kv[ty, w, pl.ds(mult(half * CH, CH), CH), :] = val
+        copy = remote(kv.at[ty, part], rbuf.at[d - 1, part], ydev(d))
+        copy.start()
+        return copy
+
+    def total(part):
+        def block(b, _):
+            for w in range(2):
+                acc4 = kv[y, part, b, w].astype(F32)
+                for d in range(3):
+                    acc4 = acc4 + rbuf[d, part, b, w].astype(F32)
+                kv[y, part, b, w] = acc4.astype(BF)
             return 0
 
-        def both(half, _):
-            all_rows(came * 2 + half, 0, g, half)
-            return 0
-
-        lax.fori_loop(0, 2, both, 0)
-        if d == 0:
-            for i in range(4):
-                for h in range(HEADS):
-                    rs = slice(h * T, (h + 1) * T)
-                    q_ref[i, :, rs] = (acc[i, rs, :T] * acc[i, rs, T:]).astype(BF)
-            for e in (2, 1, 3, 0):
-                tx = (x + e) % 4
-                copy = local if e == 0 else functools.partial(remote, dev=xdev(e))
-                homes.append(copy(q_ref.at[tx], query_grad.at[resp, :, wide(kvh)]))
-                homes[-1].start()
-        lax.fori_loop(0, 2, finish, 0)
-        if d:
-            yback.append(remote(kv.at[ty, :, front, :], rbuf.at[d - 1, :, front, :], ydev(d)))
-            yback[-1].start()
-        if d == 3:
-            for copy in yback_resp:
-                copy.wait()
-            lax.fori_loop(8, 12, total, 0)
-            for e in range(4):
-                tx = (x + e) % 4
-                copy = local if e == 0 else functools.partial(remote, dev=xdev(e))
-                for w, out in ((0, key_grad), (1, value_grad)):
-                    homes.append(copy(kv.at[y, w, blk(8 + tx), :], out.at[resp, :, hd(kvh)]))
+        lax.fori_loop(0, 4, block, 0)
+
+    yback = {2: [send_back(d, 2) for d in (2, 1, 3)], OTHER: [], OWN: []}
+    tail = []
+    for kind in (OTHER, OWN):
+        for d in (2, 1, 3, 0):
+            p = uses.index(((4 - d) % 4, kind))
+            ty, part = (y + d) % 4, half(kind)
+            scaled(p // 2)
+            all_rows(p, 0, p // 2)
+            if d == 0 and kind == OWN:
+                for i in range(4):
+                    for h in range(HEADS):
+                        rs = slice(h * T, (h + 1) * T)
+                        q_ref[i, :, rs] = (acc[i, rs, :T] * acc[i, rs, T:]).astype(BF)
+                for e in (2, 1, 3, 0):
+                    tx = (x + e) % 4
+                    copy = local if e == 0 else functools.partial(remote, dev=xdev(e))
+                    homes.append(copy(q_ref.at[tx], query_grad.at[resp, :, wide(kvh)]))
                     homes[-1].start()
-
-    for copy in yback:
-        copy.wait()
-    lax.fori_loop(0, 8, total, 0)
-    tail = []
-    for other in (1, 0):
-        for d in (2, 1, 3, 0):
-            tx, tg = (x + d) % 4, (grp + other) % 2
-            copy = local if (d == 0 and not other) else functools.partial(remote, dev=xdev(d, other))
-            tail.append(copy(kv.at[y, :, blk(tg * 4 + tx), :], pbuf.at[grp * 4 + x]))
-            tail[-1].start()
-    for copy in tail:
-        copy.wait()
+            for w, val in enumerate(keys_part(p, 0)):
+                for b in range(4):
+                    kv[ty, part, b, w] = val[b * T:(b + 1) * T]
+            if d:
+                yback[kind].append(send_back(d, part))
+            if d == 3 and kind == OTHER:
+                wait(yback[2])
+                total(2)
+                for e in range(4):
+                    tx = (x + e) % 4
+                    copy = local if e == 0 else functools.partial(remote, dev=xdev(e))
+                    for w, out in ((0, key_grad), (1, value_grad)):
+                        homes.append(copy(kv.at[y, 2, tx, w], out.at[resp, :, hd(kvh)]))
+                        homes[-1].start()
+            if d == 2 and kind == OWN:
+                wait(yback[OTHER])
+                total(half(OTHER))
+                for e in (2, 1, 3, 0):
+                    tail.append(remote(kv.at[y, half(OTHER), (x + e) % 4], pbuf.at[grp * 4 + x], xdev(e, 1)))
+                    tail[-1].start()
+
+    wait(yback[OWN])
+    total(half(OWN))
+    for e in (2, 1, 3):
+        tail.append(remote(kv.at[y, grp, (x + e) % 4], pbuf.at[grp * 4 + x], xdev(e)))
+        tail[-1].start()
+    pbuf[grp * 4 + x] = kv[y, grp, x]
+    wait(tail)
     for j in range(2):
         for w, out in ((0, pk_grad), (1, pv_grad)):
             parts = [pbuf[gg * 4 + rr * 2 + j, w].astype(F32) for gg in range(2) for rr in range(2)]
             out[:, j * T:(j + 1) * T] = (parts[0] + parts[1] + parts[2] + parts[3]).astype(BF)
-    for copy in homes:
-        copy.wait()
+    wait(homes)
     assert counter[0] <= N_SEM and counter[1] <= N_SEM
 
 
@@ -409,10 +407,10 @@
         in_specs=[pl.BlockSpec(memory_space=pltpu.SMEM)] + [hbm] * 6,
         out_specs=[hbm] * 4 + [vmem] * 2,
         scratch_shapes=[
-            V((4, T, R), BF), V((4, T, R), BF), V((4, 2, 1536, T), BF), V((3, 2, 1536, T), BF),
+            V((4, T, R), BF), V((4, T, R), BF), V((4, 3, 4, 2, T, T), BF), V((3, 3, 4, 2, T, T), BF),
             V((8, 2, T, T), BF),
             V((6144, 256), BF), V((6144, 256), BF), V((4, R, 256), BF),
-            V((2, 4, T, R), BF), V((2, T, 4 * R), BF), V((4, R, CH), F32), V((2, 4, R, CH), BF), V((42, R, CH), BF),
+            V((2, 4, T, R), BF), V((2, T, 4 * R), BF), V((4, R, CH), F32), V((4, R, CH), BF), V((42, R, CH), BF),
             V((4, R, T), F32), V((4, R, T), F32), V((4, 8, R), F32), V((R, T), F32), V((4, R, 256), F32),
             pltpu.SemaphoreType.DMA((N_SEM,)), pltpu.SemaphoreType.DMA((N_SEM,)),
             pltpu.SemaphoreType.DMA((N_SEM,)),

time: 118 us -> 121 us (1.025)
  Pallas kernels: 117 us -> 120 us
    pallas_call x1, Pallas kernels: 115 us -> 118 us  [shards(): pl.pallas_call(kernel, out_shape=shapes, in_specs=[pl.BlockSpec(memory_sp...]
where the time goes in v3:
time: 121 us
  Pallas kernels  120 us (99%)
    pallas_call x1, Pallas kernels, shards(): pl.pallas_call(kernel, out_shape=shapes, in_specs=[pl.BlockSpec(memory_sp...  118 us

profile of v3, /device:TPU:0, one launch (start us, length us, event | category | flops | bytes accessed | tf_op | source)
XLA Modules:
  0.0 120.9 jit_solution(85631362192662365)
XLA Ops:
  0.6 117.7 %attention.1 = (bf16[2,128,1280]{2,1,0:T(8,128)(2,1)}, bf16[2,128,1280]{2,1,0:T(8,128)(2,1)}, bf16[2,128,256]{2,1,0:T(8,128)(2,1)}, bf16[2,128,256]{2,1,0:T(8,12...) custom-call(s32[2]{0:T(128)} %lens_ref.1, bf16[2,128,1280]{2,1,0:T(8,128)(2,1)} %queries.1, ...), custom_call_target="tpu_custom_call" | custom-call | tf_op jit(solution)/shard_map/attention/pallas_call | solution.py:404
  118.4 2.4 %settle.1 = (bf16[2,128,1280]{2,1,0:T(8,128)(2,1)}, bf16[2,128,1280]{2,1,0:T(8,128)(2,1)}, bf16[2,128,256]{2,1,0:T(8,128)(2,1)}, bf16[2,128,256]{2,1,0:T(8,128)(...) custom-call(bf16[2,128,1280]{2,1,0:T(8,128)(2,1)} %get-tuple-element.12.refs_0_, ...), custom_call_target="tpu_custom_call" | custom-call | tf_op jit(solution)/shard_map/settle/pallas_call | solution.py:423

commit v4 on v3

--- a/solution.py
+++ b/solution.py
@@ -28,8 +28,8 @@
 def kernel(
     lens_ref, queries, keys, values, pkeys, pvalues, gout,
     attended, query_grad, key_grad, value_grad, pk_grad, pv_grad,
-    q_ref, g_ref, kv, rbuf, pbuf,
-    ka, va, qa, gt, gs, s_ref, ds_ref, e_ref, mrun, stat, turned, top_ref, acc,
+    q_ref, g_ref, kv, rbuf, zbuf, pbuf,
+    ka, va, qa, gt, gs, s_ref, ds_ref, e_ref, mrun, stat, turned, acc,
     send, recv, lsem,
 ):
     grp, ctx, head = lax.axis_index("grp"), lax.axis_index("ctx"), lax.axis_index("head")
@@ -59,7 +59,7 @@
         counter[1] += 1
         return pltpu.make_async_copy(src, dst, lsem.at[k])
 
-    partners = [xdev(d) for d in (1, 2, 3)] + [ydev(d) for d in (1, 2, 3)] + [xdev(d, 1) for d in range(4)]
+    partners = [xdev(d) for d in (1, 2, 3)] + [ydev(d) for d in (1, 2, 3)] + [xdev(0, 1)]
     barrier = pltpu.get_barrier_semaphore()
     for dev in partners:
         pl.semaphore_signal(barrier, inc=1, device_id=dev, device_id_type=MESH)
@@ -71,23 +71,18 @@
     def wide(j):
         return pl.ds(mult(j * R, T), R)
 
-    pre, own, late = [], [], []
-    for d in range(4):
-        j = (x + d) % 2
-        copy = local if d == 0 else functools.partial(remote, dev=xdev(d))
-        for which, ref in ((0, pkeys), (1, pvalues)):
-            pre.append(copy(ref.at[:, hd(j)], kv.at[y, grp, x, which]))
-    for d in range(4):
+    prompt, mine, asked, later = [], [], [], []
+    for d in (0, 2, 1, 3):
         tx = (x + d) % 4
         r, j = tx // 2, tx % 2
         copy = local if d == 0 else functools.partial(remote, dev=xdev(d))
+        for which, ref in ((0, pkeys), (1, pvalues)):
+            prompt.append(copy(ref.at[:, hd(j)], kv.at[y, grp, x, which]))
+        (asked if d else mine).append(copy(queries.at[r, :, wide(j)], q_ref.at[x]))
         for which, ref in ((0, keys), (1, values)):
-            pre.append(copy(ref.at[r, :, hd(j)], kv.at[y, 2, x, which]))
-        for ref, buf in ((queries, q_ref), (gout, g_ref)):
-            (late if d else own).append(copy(ref.at[r, :, wide(j)], buf.at[x]))
-    for copy in pre + own:
-        copy.start()
-    asked, graded = late[0::2], late[1::2]
+            (later if d else mine).append(copy(ref.at[r, :, hd(j)], kv.at[y, 2, x, which]))
+        (later if d else mine).append(copy(gout.at[r, :, wide(j)], g_ref.at[x]))
+    later = later[0::3] + later[1::3] + later[2::3]
 
     up, down = (y + 1) % 4, (y + 3) % 4
 
@@ -116,10 +111,11 @@
         for copy in copies:
             copy.wait()
 
-    wait(pre[:8])
+    start(prompt + mine + asked)
+    wait(prompt)
     start(near_prompt + swap[0])
-    wait(pre[8:])
-    start(asked)
+    wait(mine + asked)
+    start(later)
 
     OWN, OTHER = 0, 1
     uses = [(0, OWN), (0, OTHER), (1, OWN), (3, OWN), (1, OTHER), (2, OWN), (3, OTHER), (2, OTHER)]
@@ -148,10 +144,12 @@
 
     def slot(c, i):
         n = c - PC
-        return jnp.where(n < 0, 4 * c + i, 32 + 4 * n - (n * (n - 1)) // 2 + i - n)
+        if isinstance(c, int) and n >= 0:
+            return 32 + 4 * n - (n * (n - 1)) // 2 + i - n
+        return 4 * c + i
 
     def chunk_rows(c):
-        return pl.ds(mult(c * CH, CH), CH)
+        return slice(c * CH, (c + 1) * CH) if isinstance(c, int) else pl.ds(mult(c * CH, CH), CH)
 
     def fold(s):
         return functools.reduce(jnp.maximum, [s[:, k * T:(k + 1) * T] for k in range(CH // T)])
@@ -175,47 +173,30 @@
         s_ref[slot] = s
         return fold(s)
 
-    def weigh(i, base, count, g, top):
+    def weigh(i, chunks, g, top):
         old = mrun[i]
         new = jnp.maximum(old, jnp.broadcast_to(jnp.max(top, 1, keepdims=True), (R, T)))
         mrun[i] = new
         stat[i] = jnp.where(lane == g, new, stat[i])
         fade = jnp.exp2(old - new)
-        acc[i, :, :T] *= fade
-        acc[i, :, T:] *= fade
-
-        def exps(n, _):
-            c = base + n
+        acc[i] *= jnp.concatenate([fade, fade], 1)
+        for c, buf in chunks:
             mm = mrun[i]
-            s = s_ref[n]
+            s = s_ref[buf]
             e = jnp.concatenate(
                 [jnp.exp2(s[:, k * T:(k + 1) * T] - mm) for k in range(CH // T)], 1
             ).astype(BF)
             e_ref[slot(c, i)] = e
             acc[i] += dot(e, va[chunk_rows(c), :], NN)
-            return 0
-
-        lax.fori_loop(0, count, exps, 0)
 
     def prefix_group(g):
-        place(2 * g)
-        place(2 * g + 1)
-
-        def tile(i, _):
-            top = jnp.maximum(scores(i, 2 * g, 0), scores(i, 2 * g + 1, 1))
-            weigh(i, 2 * g, 2, g, top)
-            return 0
-
-        lax.fori_loop(0, 4, tile, 0)
-
-    def response_tile(i, _):
-        top_ref[...] = jnp.full((R, T), -jnp.inf, F32)
-
-        def one(n, _):
-            top_ref[...] = jnp.maximum(top_ref[...], scores(i, PC + n, n))
-            return 0
-
-        lax.fori_loop(0, i, one, 0)
+        for i in range(4):
+            chunks = [(2 * g + n, (i % 2) * 2 + n) for n in range(2)]
+            top = functools.reduce(jnp.maximum, [scores(i, c, buf) for c, buf in chunks])
+            weigh(i, chunks, g, top)
+
+    def response_tile(i):
+        tops = [scores(i, PC + n, n) for n in range(i)]
         s = dot(qa[i], ka[chunk_rows(PC + i), :], NT)
         col = lax.broadcasted_iota(jnp.int32, (T, CH), 1)
         row = lax.broadcasted_iota(jnp.int32, (T, CH), 0) + y * T
@@ -224,7 +205,8 @@
             [jnp.where(seen, s[h * T:(h + 1) * T], -jnp.inf) for h in range(HEADS)], 0
         )
         s_ref[i] = s
-        weigh(i, PC, i + 1, 4, jnp.maximum(top_ref[...], fold(s)))
+        tops.append(fold(s))
+        weigh(i, [(PC + n, n) for n in range(i + 1)], 4, functools.reduce(jnp.maximum, tops))
         stat[i] = jnp.exp2(stat[i] - mrun[i])
         pos = lax.broadcasted_iota(jnp.int32, (T, T), 0) + (i * CH + y * T)
         live = pos < lens_ref[resp]
@@ -248,27 +230,49 @@
             turned[i, :, rs] = stat[i, rs, :].T[:8]
             acc[i, rs, T:] = inv * scale
         acc[i, :, :T] = jnp.zeros((R, T), F32)
+
+    lax.fori_loop(0, 4, prepare, 0)
+
+    def group(g, _):
+        @pl.when(g == 0)
+        def _():
+            wait(near_prompt + swap[0])
+            start(swap[1] + far_prompt)
+            place(0)
+            place(1)
+
+        @pl.when(g == 1)
+        def _():
+            wait(later)
+            start(near_resp)
+            wait(swap[1])
+            start(swap[3])
+            place(2)
+            place(3)
+
+        @pl.when(g == 2)
+        def _():
+            wait(far_prompt)
+            start(swap[2])
+            wait(near_resp)
+            start(far_resp)
+            place(4)
+            place(5)
+
+        @pl.when(g == 3)
+        def _():
+            wait(swap[3] + swap[2])
+            place(6)
+            place(7)
+
+        prefix_group(g)
         return 0
 
-    wait(own + asked)
-    start(graded)
-    lax.fori_loop(0, 4, prepare, 0)
-    wait(near_prompt + swap[0])
-    start(swap[1] + far_prompt + near_resp)
-    prefix_group(0)
-    wait(swap[1])
-    start(swap[3])
-    prefix_group(1)
-    wait(far_prompt)
-    start(swap[2])
-    wait(near_resp)
-    start(far_resp)
-    prefix_group(2)
-    wait(swap[3] + swap[2])
-    prefix_group(3)
-    wait(far_resp + graded)
+    lax.fori_loop(0, 4, group, 0)
+    wait(far_resp)
     place_response()
-    lax.fori_loop(0, 4, response_tile, 0)
+    for i in range(4):
+        response_tile(i)
 
     homes = []
     for d in range(4):
@@ -280,7 +284,7 @@
 
     def scaled(g):
         for i in range(4):
-            f = turned[i, g:g + 1, :]
+            f = turned[i, pl.ds(g, 1), :]
             for w in range(2):
                 gs[w, :, i * R:(i + 1) * R] = (gt[w, i].astype(F32) * f).astype(BF)
 
@@ -289,7 +293,8 @@
         dp = dot(qa[i], va[kk, :], NT)
         ds = (e_ref[slot(c, i)].astype(F32) * dp).astype(BF)
         ds_ref[i] = ds
-        acc[i, :, :T] += stat[i, :, g:g + 1] * dot(ds, ka[kk, :T], NN)
+        f = jnp.sum(jnp.where(lane == g, stat[i], 0.0), 1, keepdims=True)
+        acc[i, :, :T] += f * dot(ds, ka[kk, :T], NN)
 
     def keys_part(c, first):
         n = (4 - first) * R
@@ -301,7 +306,8 @@
         return dk.T.astype(BF), dv.T.astype(BF)
 
     def all_rows(c, first, g):
-        lax.fori_loop(first, 4, lambda i, _: (rows_part(i, c, g), 0)[1], 0)
+        for i in range(first, 4):
+            rows_part(i, c, g)
 
     scaled(4)
     for i in range(4):
@@ -312,72 +318,91 @@
 
     def send_back(d, part):
         ty = (y + d) % 4
-        copy = remote(kv.at[ty, part], rbuf.at[d - 1, part], ydev(d))
-        copy.start()
-        return copy
-
-    def total(part):
+        return remote(kv.at[ty, part], rbuf.at[d - 1, part], ydev(d))
+
+    def total(part, extra=None):
         def block(b, _):
             for w in range(2):
                 acc4 = kv[y, part, b, w].astype(F32)
                 for d in range(3):
                     acc4 = acc4 + rbuf[d, part, b, w].astype(F32)
+                if extra is not None:
+                    acc4 = acc4 + extra[b, w].astype(F32)
                 kv[y, part, b, w] = acc4.astype(BF)
             return 0
 
         lax.fori_loop(0, 4, block, 0)
 
-    yback = {2: [send_back(d, 2) for d in (2, 1, 3)], OTHER: [], OWN: []}
-    tail = []
-    for kind in (OTHER, OWN):
-        for d in (2, 1, 3, 0):
-            p = uses.index(((4 - d) % 4, kind))
-            ty, part = (y + d) % 4, half(kind)
-            scaled(p // 2)
-            all_rows(p, 0, p // 2)
-            if d == 0 and kind == OWN:
-                for i in range(4):
-                    for h in range(HEADS):
-                        rs = slice(h * T, (h + 1) * T)
-                        q_ref[i, :, rs] = (acc[i, rs, :T] * acc[i, rs, T:]).astype(BF)
-                for e in (2, 1, 3, 0):
-                    tx = (x + e) % 4
-                    copy = local if e == 0 else functools.partial(remote, dev=xdev(e))
-                    homes.append(copy(q_ref.at[tx], query_grad.at[resp, :, wide(kvh)]))
-                    homes[-1].start()
-            for w, val in enumerate(keys_part(p, 0)):
-                for b in range(4):
-                    kv[ty, part, b, w] = val[b * T:(b + 1) * T]
-            if d:
-                yback[kind].append(send_back(d, part))
-            if d == 3 and kind == OTHER:
-                wait(yback[2])
-                total(2)
-                for e in range(4):
-                    tx = (x + e) % 4
-                    copy = local if e == 0 else functools.partial(remote, dev=xdev(e))
-                    for w, out in ((0, key_grad), (1, value_grad)):
-                        homes.append(copy(kv.at[y, 2, tx, w], out.at[resp, :, hd(kvh)]))
-                        homes[-1].start()
-            if d == 2 and kind == OWN:
-                wait(yback[OTHER])
-                total(half(OTHER))
-                for e in (2, 1, 3, 0):
-                    tail.append(remote(kv.at[y, half(OTHER), (x + e) % 4], pbuf.at[grp * 4 + x], xdev(e, 1)))
-                    tail[-1].start()
-
-    wait(yback[OWN])
-    total(half(OWN))
-    for e in (2, 1, 3):
-        tail.append(remote(kv.at[y, grp, (x + e) % 4], pbuf.at[grp * 4 + x], xdev(e)))
-        tail[-1].start()
-    pbuf[grp * 4 + x] = kv[y, grp, x]
+    hops = (2, 1, 3, 0)
+    yback = {part: [send_back(d, half(part) if part < 2 else 2) for d in (2, 1, 3)] for part in (2, OTHER, OWN)}
+    crossing = [remote(kv.at[y, half(OTHER)], zbuf, xdev(0, 1))]
+    kept, asks = [], []
+    for e in (2, 1, 3, 0):
+        tx = (x + e) % 4
+        copy = local if e == 0 else functools.partial(remote, dev=xdev(e))
+        asks.append(copy(q_ref.at[tx], query_grad.at[resp, :, wide(kvh)]))
+        for w, out in ((0, key_grad), (1, value_grad)):
+            kept.append(copy(kv.at[y, 2, tx, w], out.at[resp, :, hd(kvh)]))
+    start(yback[2])
+
+    def put(p, ty, part):
+        for w, val in enumerate(keys_part(p, 0)):
+            for b in range(4):
+                kv[ty, part, b, w] = val[b * T:(b + 1) * T]
+
+    spots = [uses.index(((4 - d) % 4, kind)) for kind in (OTHER, OWN) for d in hops]
+
+    def pick(n, table):
+        return functools.reduce(lambda v, k: jnp.where(n == k, table[k], v), range(1, len(table)), table[0])
+
+    def prompt_chunk(n, _):
+        p = pick(n, spots)
+        ty = (y + pick(n, hops * 2)) % 4
+        part = half(jnp.where(n < 4, OTHER, OWN))
+        scaled(p // 2)
+        for i in range(4):
+            rows_part(i, p, p // 2)
+        put(p, ty, part)
+        for k in range(7):
+            if k != 3:
+                @pl.when(n == k)
+                def _():
+                    yback[OTHER if k < 4 else OWN][k % 4].start()
+
+        @pl.when(n == 2)
+        def _():
+            wait(yback[2])
+            total(2)
+            start(kept)
+
+        @pl.when(n == 4)
+        def _():
+            wait(yback[OTHER])
+            total(half(OTHER))
+            start(crossing)
+
+        return 0
+
+    lax.fori_loop(0, 7, prompt_chunk, 0)
+    scaled(spots[7] // 2)
+    for i in range(4):
+        rows_part(i, spots[7], spots[7] // 2)
+    for i in range(4):
+        for h in range(HEADS):
+            rs = slice(h * T, (h + 1) * T)
+            q_ref[i, :, rs] = (acc[i, rs, :T] * acc[i, rs, T:]).astype(BF)
+    start(asks)
+    put(spots[7], y, grp)
+    wait(crossing + yback[OWN])
+    total(grp, zbuf)
+    tail = [remote(kv.at[y, grp, (x + e) % 4], pbuf.at[x], xdev(e)) for e in (2, 1, 3)]
+    start(tail)
+    pbuf[x] = kv[y, grp, x]
     wait(tail)
     for j in range(2):
         for w, out in ((0, pk_grad), (1, pv_grad)):
-            parts = [pbuf[gg * 4 + rr * 2 + j, w].astype(F32) for gg in range(2) for rr in range(2)]
-            out[:, j * T:(j + 1) * T] = (parts[0] + parts[1] + parts[2] + parts[3]).astype(BF)
-    wait(homes)
+            out[:, j * T:(j + 1) * T] = (pbuf[j, w].astype(F32) + pbuf[2 + j, w].astype(F32)).astype(BF)
+    wait(homes + kept + asks)
     assert counter[0] <= N_SEM and counter[1] <= N_SEM
 
 
@@ -408,10 +433,10 @@
         out_specs=[hbm] * 4 + [vmem] * 2,
         scratch_shapes=[
             V((4, T, R), BF), V((4, T, R), BF), V((4, 3, 4, 2, T, T), BF), V((3, 3, 4, 2, T, T), BF),
-            V((8, 2, T, T), BF),
+            V((4, 2, T, T), BF), V((4, 2, T, T), BF),
             V((6144, 256), BF), V((6144, 256), BF), V((4, R, 256), BF),
             V((2, 4, T, R), BF), V((2, T, 4 * R), BF), V((4, R, CH), F32), V((4, R, CH), BF), V((42, R, CH), BF),
-            V((4, R, T), F32), V((4, R, T), F32), V((4, 8, R), F32), V((R, T), F32), V((4, R, 256), F32),
+            V((4, R, T), F32), V((4, R, T), F32), V((4, 8, R), F32), V((4, R, 256), F32),
             pltpu.SemaphoreType.DMA((N_SEM,)), pltpu.SemaphoreType.DMA((N_SEM,)),
             pltpu.SemaphoreType.DMA((N_SEM,)),
         ],

time: 121 us -> 111 us (0.917)
  Pallas kernels: 120 us -> 110 us
    pallas_call x1, Pallas kernels: 118 us -> 107 us  [shards(): pl.pallas_call(kernel, out_shape=shapes, in_specs=[pl.BlockSpec(memory_sp...]
where the time goes in v4:
time: 111 us
  Pallas kernels  110 us (99%)
    pallas_call x1, Pallas kernels, shards(): pl.pallas_call(kernel, out_shape=shapes, in_specs=[pl.BlockSpec(memory_sp...  107 us
    pallas_call x1, Pallas kernels, shards(): pl.pallas_call(settle, out_shape=shapes, in_specs=[hbm] * 6, out_specs=[h...  2.36 us

profile of v4, /device:TPU:0, one launch (start us, length us, event | category | flops | bytes accessed | tf_op | source)
XLA Modules:
  0.0 110.6 jit_solution(3509504570679470667)
XLA Ops:
  0.6 107.4 %attention.1 = (bf16[2,128,1280]{2,1,0:T(8,128)(2,1)}, bf16[2,128,1280]{2,1,0:T(8,128)(2,1)}, bf16[2,128,256]{2,1,0:T(8,128)(2,1)}, bf16[2,128,256]{2,1,0:T(8,12...) custom-call(s32[2]{0:T(128)} %lens_ref.1, bf16[2,128,1280]{2,1,0:T(8,128)(2,1)} %queries.1, ...), custom_call_target="tpu_custom_call" | custom-call | tf_op jit(solution)/shard_map/attention/pallas_call | solution.py:429
  108.0 2.4 %settle.1 = (bf16[2,128,1280]{2,1,0:T(8,128)(2,1)}, bf16[2,128,1280]{2,1,0:T(8,128)(2,1)}, bf16[2,128,256]{2,1,0:T(8,128)(2,1)}, bf16[2,128,256]{2,1,0:T(8,128)(...) custom-call(bf16[2,128,1280]{2,1,0:T(8,128)(2,1)} %get-tuple-element.12.refs_0_, ...), custom_call_target="tpu_custom_call" | custom-call | tf_op jit(solution)/shard_map/settle/pallas_call | solution.py:448

commit v5 on v4

--- a/solution.py
+++ b/solution.py
@@ -71,7 +71,7 @@
     def wide(j):
         return pl.ds(mult(j * R, T), R)
 
-    prompt, mine, asked, later = [], [], [], []
+    prompt, mine, asked, given, graded = [], [], [], [], []
     for d in (0, 2, 1, 3):
         tx = (x + d) % 4
         r, j = tx // 2, tx % 2
@@ -80,9 +80,8 @@
             prompt.append(copy(ref.at[:, hd(j)], kv.at[y, grp, x, which]))
         (asked if d else mine).append(copy(queries.at[r, :, wide(j)], q_ref.at[x]))
         for which, ref in ((0, keys), (1, values)):
-            (later if d else mine).append(copy(ref.at[r, :, hd(j)], kv.at[y, 2, x, which]))
-        (later if d else mine).append(copy(gout.at[r, :, wide(j)], g_ref.at[x]))
-    later = later[0::3] + later[1::3] + later[2::3]
+            given.append(copy(ref.at[r, :, hd(j)], kv.at[y, 2, x, which]))
+        (graded if d else mine).append(copy(gout.at[r, :, wide(j)], g_ref.at[x]))
 
     up, down = (y + 1) % 4, (y + 3) % 4
 
@@ -111,11 +110,11 @@
         for copy in copies:
             copy.wait()
 
-    start(prompt + mine + asked)
+    start(prompt + given + mine)
     wait(prompt)
-    start(near_prompt + swap[0])
-    wait(mine + asked)
-    start(later)
+    start(near_prompt + swap[0] + asked)
+    wait(given + mine + asked)
+    start(graded)
 
     OWN, OTHER = 0, 1
     uses = [(0, OWN), (0, OTHER), (1, OWN), (3, OWN), (1, OTHER), (2, OWN), (3, OTHER), (2, OTHER)]
@@ -193,7 +192,7 @@
         for i in range(4):
             chunks = [(2 * g + n, (i % 2) * 2 + n) for n in range(2)]
             top = functools.reduce(jnp.maximum, [scores(i, c, buf) for c, buf in chunks])
-            weigh(i, chunks, g, top)
+            weigh(i, chunks, g + g // 3, top)
 
     def response_tile(i):
         tops = [scores(i, PC + n, n) for n in range(i)]
@@ -206,7 +205,9 @@
         )
         s_ref[i] = s
         tops.append(fold(s))
-        weigh(i, [(PC + n, n) for n in range(i + 1)], 4, functools.reduce(jnp.maximum, tops))
+        weigh(i, [(PC + n, n) for n in range(i + 1)], 3, functools.reduce(jnp.maximum, tops))
+
+    def conclude(i):
         stat[i] = jnp.exp2(stat[i] - mrun[i])
         pos = lax.broadcasted_iota(jnp.int32, (T, T), 0) + (i * CH + y * T)
         live = pos < lens_ref[resp]
@@ -243,10 +244,7 @@
 
         @pl.when(g == 1)
         def _():
-            wait(later)
-            start(near_resp)
-            wait(swap[1])
-            start(swap[3])
+            start(near_resp + swap[3])
             place(2)
             place(3)
 
@@ -254,13 +252,17 @@
         def _():
             wait(far_prompt)
             start(swap[2])
-            wait(near_resp)
+            wait(near_resp + swap[1])
             start(far_resp)
             place(4)
             place(5)
 
         @pl.when(g == 3)
         def _():
+            wait(far_resp)
+            place_response()
+            for i in range(4):
+                response_tile(i)
             wait(swap[3] + swap[2])
             place(6)
             place(7)
@@ -269,10 +271,9 @@
         return 0
 
     lax.fori_loop(0, 4, group, 0)
-    wait(far_resp)
-    place_response()
+    wait(graded)
     for i in range(4):
-        response_tile(i)
+        conclude(i)
 
     homes = []
     for d in range(4):
@@ -309,33 +310,40 @@
         for i in range(first, 4):
             rows_part(i, c, g)
 
-    scaled(4)
+    scaled(3)
     for i in range(4):
-        all_rows(PC + i, i, 4)
+        all_rows(PC + i, i, 3)
         for w, val in enumerate(keys_part(PC + i, i)):
             for b in range(4):
                 kv[b, 2, i, w] = val[b * T:(b + 1) * T]
 
-    def send_back(d, part):
+    def send_back(d, part, place):
         ty = (y + d) % 4
-        return remote(kv.at[ty, part], rbuf.at[d - 1, part], ydev(d))
-
-    def total(part, extra=None):
+        return remote(kv.at[ty, part], rbuf.at[d - 1, place], ydev(d))
+
+    def total(part, place):
         def block(b, _):
             for w in range(2):
                 acc4 = kv[y, part, b, w].astype(F32)
                 for d in range(3):
-                    acc4 = acc4 + rbuf[d, part, b, w].astype(F32)
-                if extra is not None:
-                    acc4 = acc4 + extra[b, w].astype(F32)
+                    acc4 = acc4 + rbuf[d, place, b, w].astype(F32)
                 kv[y, part, b, w] = acc4.astype(BF)
             return 0
 
         lax.fori_loop(0, 4, block, 0)
 
+    def join(ty):
+        for b in range(4):
+            for w in range(2):
+                kv[ty, grp, b, w] = (kv[ty, grp, b, w].astype(F32) + zbuf[ty, b, w].astype(F32)).astype(BF)
+
     hops = (2, 1, 3, 0)
-    yback = {part: [send_back(d, half(part) if part < 2 else 2) for d in (2, 1, 3)] for part in (2, OTHER, OWN)}
-    crossing = [remote(kv.at[y, half(OTHER)], zbuf, xdev(0, 1))]
+    back_resp = [send_back(d, 2, 0) for d in (2, 1, 3)]
+    back_prompt = [send_back(d, grp, 1) for d in (2, 1, 3)]
+    crossing = []
+    for d in hops:
+        ty = (y + d) % 4
+        crossing.append(remote(kv.at[ty, half(OTHER)], zbuf.at[ty], xdev(0, 1)))
     kept, asks = [], []
     for e in (2, 1, 3, 0):
         tx = (x + e) % 4
@@ -343,7 +351,7 @@
         asks.append(copy(q_ref.at[tx], query_grad.at[resp, :, wide(kvh)]))
         for w, out in ((0, key_grad), (1, value_grad)):
             kept.append(copy(kv.at[y, 2, tx, w], out.at[resp, :, hd(kvh)]))
-    start(yback[2])
+    start(back_resp)
 
     def put(p, ty, part):
         for w, val in enumerate(keys_part(p, 0)):
@@ -359,27 +367,28 @@
         p = pick(n, spots)
         ty = (y + pick(n, hops * 2)) % 4
         part = half(jnp.where(n < 4, OTHER, OWN))
-        scaled(p // 2)
+        g = p // 2 + p // 6
+        scaled(g)
         for i in range(4):
-            rows_part(i, p, p // 2)
+            rows_part(i, p, g)
         put(p, ty, part)
-        for k in range(7):
-            if k != 3:
-                @pl.when(n == k)
-                def _():
-                    yback[OTHER if k < 4 else OWN][k % 4].start()
-
-        @pl.when(n == 2)
+        for k in range(4):
+            @pl.when(n == k)
+            def _():
+                crossing[k].start()
+
+        for k in range(3):
+            @pl.when(n == 4 + k)
+            def _():
+                crossing[k].wait()
+                join(ty)
+                back_prompt[k].start()
+
+        @pl.when(n == 3)
         def _():
-            wait(yback[2])
-            total(2)
+            wait(back_resp)
+            total(2, 0)
             start(kept)
-
-        @pl.when(n == 4)
-        def _():
-            wait(yback[OTHER])
-            total(half(OTHER))
-            start(crossing)
 
         return 0
 
@@ -393,8 +402,10 @@
             q_ref[i, :, rs] = (acc[i, rs, :T] * acc[i, rs, T:]).astype(BF)
     start(asks)
     put(spots[7], y, grp)
-    wait(crossing + yback[OWN])
-    total(grp, zbuf)
+    crossing[3].wait()
+    join(y)
+    wait(back_prompt)
+    total(grp, 1)
     tail = [remote(kv.at[y, grp, (x + e) % 4], pbuf.at[x], xdev(e)) for e in (2, 1, 3)]
     start(tail)
     pbuf[x] = kv[y, grp, x]
@@ -432,8 +443,8 @@
         in_specs=[pl.BlockSpec(memory_space=pltpu.SMEM)] + [hbm] * 6,
         out_specs=[hbm] * 4 + [vmem] * 2,
         scratch_shapes=[
-            V((4, T, R), BF), V((4, T, R), BF), V((4, 3, 4, 2, T, T), BF), V((3, 3, 4, 2, T, T), BF),
-            V((4, 2, T, T), BF), V((4, 2, T, T), BF),
+            V((4, T, R), BF), V((4, T, R), BF), V((4, 3, 4, 2, T, T), BF), V((3, 2, 4, 2, T, T), BF),
+            V((4, 4, 2, T, T), BF), V((4, 2, T, T), BF),
             V((6144, 256), BF), V((6144, 256), BF), V((4, R, 256), BF),
             V((2, 4, T, R), BF), V((2, T, 4 * R), BF), V((4, R, CH), F32), V((4, R, CH), BF), V((42, R, CH), BF),
             V((4, R, T), F32), V((4, R, T), F32), V((4, 8, R), F32), V((4, R, 256), F32),

time: 111 us -> 95.5 us (0.86)
  Pallas kernels: 110 us -> 94.4 us
    pallas_call x1, Pallas kernels: 107 us -> 92 us  [shards(): pl.pallas_call(kernel, out_shape=shapes, in_specs=[pl.BlockSpec(memory_sp...]
where the time goes in v5:
time: 95.5 us; the launch traced here: 95.2 us
  Pallas kernels  94.4 us (99%)
    pallas_call x1, Pallas kernels, shards(): pl.pallas_call(kernel, out_shape=shapes, in_specs=[pl.BlockSpec(memory_sp...  92 us
    pallas_call x1, Pallas kernels, shards(): pl.pallas_call(settle, out_shape=shapes, in_specs=[hbm] * 6, out_specs=[h...  2.36 us

profile of v5, /device:TPU:0, one launch (start us, length us, event | category | flops | bytes accessed | tf_op | source)
XLA Modules:
  0.0 95.2 jit_solution(14341987657360616499)
XLA Ops:
  0.6 92.0 %attention.1 = (bf16[2,128,1280]{2,1,0:T(8,128)(2,1)}, bf16[2,128,1280]{2,1,0:T(8,128)(2,1)}, bf16[2,128,256]{2,1,0:T(8,128)(2,1)}, bf16[2,128,256]{2,1,0:T(8,12...) custom-call(s32[2]{0:T(128)} %lens_ref.1, bf16[2,128,1280]{2,1,0:T(8,128)(2,1)} %queries.1, ...), custom_call_target="tpu_custom_call" | custom-call | tf_op jit(solution)/shard_map/attention/pallas_call | solution.py:440
  92.6 2.4 %settle.1 = (bf16[2,128,1280]{2,1,0:T(8,128)(2,1)}, bf16[2,128,1280]{2,1,0:T(8,128)(2,1)}, bf16[2,128,256]{2,1,0:T(8,128)(2,1)}, bf16[2,128,256]{2,1,0:T(8,128)(...) custom-call(bf16[2,128,1280]{2,1,0:T(8,128)(2,1)} %get-tuple-element.12.refs_0_, ...), custom_call_target="tpu_custom_call" | custom-call | tf_op jit(solution)/shard_map/settle/pallas_call | solution.py:459

commit v6 on v5

--- a/solution.py
+++ b/solution.py
@@ -110,11 +110,13 @@
         for copy in copies:
             copy.wait()
 
-    start(prompt + given + mine)
+    start(prompt + mine)
     wait(prompt)
     start(near_prompt + swap[0] + asked)
-    wait(given + mine + asked)
-    start(graded)
+    wait(near_prompt)
+    start(swap[1] + far_prompt)
+    wait(mine + asked)
+    start(given)
 
     OWN, OTHER = 0, 1
     uses = [(0, OWN), (0, OTHER), (1, OWN), (3, OWN), (1, OTHER), (2, OWN), (3, OTHER), (2, OTHER)]
@@ -237,23 +239,25 @@
     def group(g, _):
         @pl.when(g == 0)
         def _():
-            wait(near_prompt + swap[0])
-            start(swap[1] + far_prompt)
+            wait(swap[0])
+            start(swap[3])
             place(0)
             place(1)
 
         @pl.when(g == 1)
         def _():
-            start(near_resp + swap[3])
+            wait(given)
+            start(near_resp + graded)
+            wait(far_prompt)
+            start(swap[2])
             place(2)
             place(3)
 
         @pl.when(g == 2)
         def _():
-            wait(far_prompt)
-            start(swap[2])
-            wait(near_resp + swap[1])
+            wait(near_resp)
             start(far_resp)
+            wait(swap[1])
             place(4)
             place(5)
 
@@ -310,12 +314,13 @@
         for i in range(first, 4):
             rows_part(i, c, g)
 
-    scaled(3)
-    for i in range(4):
-        all_rows(PC + i, i, 3)
-        for w, val in enumerate(keys_part(PC + i, i)):
-            for b in range(4):
-                kv[b, 2, i, w] = val[b * T:(b + 1) * T]
+    def response_chunks():
+        scaled(3)
+        for i in range(4):
+            all_rows(PC + i, i, 3)
+            for w, val in enumerate(keys_part(PC + i, i)):
+                for b in range(4):
+                    kv[b, 2, i, w] = val[b * T:(b + 1) * T]
 
     def send_back(d, part, place):
         ty = (y + d) % 4
@@ -351,7 +356,6 @@
         asks.append(copy(q_ref.at[tx], query_grad.at[resp, :, wide(kvh)]))
         for w, out in ((0, key_grad), (1, value_grad)):
             kept.append(copy(kv.at[y, 2, tx, w], out.at[resp, :, hd(kvh)]))
-    start(back_resp)
 
     def put(p, ty, part):
         for w, val in enumerate(keys_part(p, 0)):
@@ -367,6 +371,12 @@
         p = pick(n, spots)
         ty = (y + pick(n, hops * 2)) % 4
         part = half(jnp.where(n < 4, OTHER, OWN))
+
+        @pl.when(n == 1)
+        def _():
+            response_chunks()
+            start(back_resp)
+
         g = p // 2 + p // 6
         scaled(g)
         for i in range(4):
@@ -384,7 +394,7 @@
                 join(ty)
                 back_prompt[k].start()
 
-        @pl.when(n == 3)
+        @pl.when(n == 5)
         def _():
             wait(back_resp)
             total(2, 0)

time: 95.5 us -> 91.9 us (0.962)
  Pallas kernels: 94.4 us -> 90.8 us
    pallas_call x1, Pallas kernels: 92 us -> 88.4 us  [shards(): pl.pallas_call(kernel, out_shape=shapes, in_specs=[pl.BlockSpec(memory_sp...]
where the time goes in v6:
time: 91.9 us; the launch traced here: 91.6 us
  Pallas kernels  90.8 us (99%)
    pallas_call x1, Pallas kernels, shards(): pl.pallas_call(kernel, out_shape=shapes, in_specs=[pl.BlockSpec(memory_sp...  88.4 us
    pallas_call x1, Pallas kernels, shards(): pl.pallas_call(settle, out_shape=shapes, in_specs=[hbm] * 6, out_specs=[h...  2.36 us

profile of v6, /device:TPU:0, one launch (start us, length us, event | category | flops | bytes accessed | tf_op | source)
XLA Modules:
  0.0 91.6 jit_solution(11362336007085963050)
XLA Ops:
  0.6 88.4 %attention.1 = (bf16[2,128,1280]{2,1,0:T(8,128)(2,1)}, bf16[2,128,1280]{2,1,0:T(8,128)(2,1)}, bf16[2,128,256]{2,1,0:T(8,128)(2,1)}, bf16[2,128,256]{2,1,0:T(8,12...) custom-call(s32[2]{0:T(128)} %lens_ref.1, bf16[2,128,1280]{2,1,0:T(8,128)(2,1)} %queries.1, ...), custom_call_target="tpu_custom_call" | custom-call | tf_op jit(solution)/shard_map/attention/pallas_call | solution.py:450
  89.1 2.4 %settle.1 = (bf16[2,128,1280]{2,1,0:T(8,128)(2,1)}, bf16[2,128,1280]{2,1,0:T(8,128)(2,1)}, bf16[2,128,256]{2,1,0:T(8,128)(2,1)}, bf16[2,128,256]{2,1,0:T(8,128)(...) custom-call(bf16[2,128,1280]{2,1,0:T(8,128)(2,1)} %get-tuple-element.12.refs_0_, ...), custom_call_target="tpu_custom_call" | custom-call | tf_op jit(solution)/shard_map/settle/pallas_call | solution.py:469

commit v7 on v6

--- a/solution.py
+++ b/solution.py
@@ -115,8 +115,6 @@
     start(near_prompt + swap[0] + asked)
     wait(near_prompt)
     start(swap[1] + far_prompt)
-    wait(mine + asked)
-    start(given)
 
     OWN, OTHER = 0, 1
     uses = [(0, OWN), (0, OTHER), (1, OWN), (3, OWN), (1, OTHER), (2, OWN), (3, OTHER), (2, OTHER)]
@@ -164,6 +162,9 @@
             hi = qs.astype(BF)
             qa[i, rs, :T] = hi
             qa[i, rs, T:] = (qs - hi.astype(F32)).astype(BF)
+        return 0
+
+    def clear(i, _):
         acc[i] = jnp.zeros((R, 2 * T), F32)
         mrun[i] = jnp.full((R, T), -jnp.inf, F32)
         stat[i] = jnp.zeros((R, T), F32)
@@ -180,15 +181,17 @@
         mrun[i] = new
         stat[i] = jnp.where(lane == g, new, stat[i])
         fade = jnp.exp2(old - new)
-        acc[i] *= jnp.concatenate([fade, fade], 1)
+        es = []
         for c, buf in chunks:
-            mm = mrun[i]
             s = s_ref[buf]
             e = jnp.concatenate(
-                [jnp.exp2(s[:, k * T:(k + 1) * T] - mm) for k in range(CH // T)], 1
+                [jnp.exp2(s[:, k * T:(k + 1) * T] - new) for k in range(CH // T)], 1
             ).astype(BF)
             e_ref[slot(c, i)] = e
-            acc[i] += dot(e, va[chunk_rows(c), :], NN)
+            es.append(e)
+        first = chunks[0][0] * CH
+        keys_in = pl.ds(first if isinstance(first, int) else mult(first, CH), CH * len(chunks))
+        acc[i] = acc[i] * jnp.concatenate([fade, fade], 1) + dot(jnp.concatenate(es, 1), va[keys_in, :], NN)
 
     def prefix_group(g):
         for i in range(4):
@@ -234,6 +237,9 @@
             acc[i, rs, T:] = inv * scale
         acc[i, :, :T] = jnp.zeros((R, T), F32)
 
+    lax.fori_loop(0, 4, clear, 0)
+    wait(mine + asked)
+    start(given)
     lax.fori_loop(0, 4, prepare, 0)
 
     def group(g, _):
@@ -326,16 +332,15 @@
         ty = (y + d) % 4
         return remote(kv.at[ty, part], rbuf.at[d - 1, place], ydev(d))
 
+    def sum_block(b, part, place):
+        for w in range(2):
+            acc4 = kv[y, part, b, w].astype(F32)
+            for d in range(3):
+                acc4 = acc4 + rbuf[d, place, b, w].astype(F32)
+            kv[y, part, b, w] = acc4.astype(BF)
+
     def total(part, place):
-        def block(b, _):
-            for w in range(2):
-                acc4 = kv[y, part, b, w].astype(F32)
-                for d in range(3):
-                    acc4 = acc4 + rbuf[d, place, b, w].astype(F32)
-                kv[y, part, b, w] = acc4.astype(BF)
-            return 0
-
-        lax.fori_loop(0, 4, block, 0)
+        lax.fori_loop(0, 4, lambda b, _: (sum_block(b, part, place), 0)[1], 0)
 
     def join(ty):
         for b in range(4):
@@ -415,9 +420,11 @@
     crossing[3].wait()
     join(y)
     wait(back_prompt)
-    total(grp, 1)
     tail = [remote(kv.at[y, grp, (x + e) % 4], pbuf.at[x], xdev(e)) for e in (2, 1, 3)]
-    start(tail)
+    for e, copy in zip((2, 1, 3), tail):
+        sum_block((x + e) % 4, grp, 1)
+        copy.start()
+    sum_block(x, grp, 1)
     pbuf[x] = kv[y, grp, x]
     wait(tail)
     for j in range(2):

time: 91.9 us -> 91.7 us (level)
  no operation moved by 1% of the time
where the time goes in v7:
time: 91.7 us; the launch traced here: 91.1 us
  Pallas kernels  90.3 us (98%)
    pallas_call x1, Pallas kernels, shards(): pl.pallas_call(kernel, out_shape=shapes, in_specs=[pl.BlockSpec(memory_sp...  88 us
    pallas_call x1, Pallas kernels, shards(): pl.pallas_call(settle, out_shape=shapes, in_specs=[hbm] * 6, out_specs=[h...  2.36 us

profile of v7, /device:TPU:0, one launch (start us, length us, event | category | flops | bytes accessed | tf_op | source)
XLA Modules:
  0.0 91.1 jit_solution(4873161954244090987)
XLA Ops:
  0.6 88.0 %attention.1 = (bf16[2,128,1280]{2,1,0:T(8,128)(2,1)}, bf16[2,128,1280]{2,1,0:T(8,128)(2,1)}, bf16[2,128,256]{2,1,0:T(8,128)(2,1)}, bf16[2,128,256]{2,1,0:T(8,12...) custom-call(s32[2]{0:T(128)} %lens_ref.1, bf16[2,128,1280]{2,1,0:T(8,128)(2,1)} %queries.1, ...), custom_call_target="tpu_custom_call" | custom-call | tf_op jit(solution)/shard_map/attention/pallas_call | solution.py:457
  88.6 2.4 %settle.1 = (bf16[2,128,1280]{2,1,0:T(8,128)(2,1)}, bf16[2,128,1280]{2,1,0:T(8,128)(2,1)}, bf16[2,128,256]{2,1,0:T(8,128)(2,1)}, bf16[2,128,256]{2,1,0:T(8,128)(...) custom-call(bf16[2,128,1280]{2,1,0:T(8,128)(2,1)} %get-tuple-element.12.refs_0_, ...), custom_call_target="tpu_custom_call" | custom-call | tf_op jit(solution)/shard_map/settle/pallas_call | solution.py:476

commit v8 on v7

--- a/solution.py
+++ b/solution.py
@@ -114,7 +114,7 @@
     wait(prompt)
     start(near_prompt + swap[0] + asked)
     wait(near_prompt)
-    start(swap[1] + far_prompt)
+    start(swap[1] + far_prompt + given)
 
     OWN, OTHER = 0, 1
     uses = [(0, OWN), (0, OTHER), (1, OWN), (3, OWN), (1, OTHER), (2, OWN), (3, OTHER), (2, OTHER)]
@@ -239,7 +239,6 @@
 
     lax.fori_loop(0, 4, clear, 0)
     wait(mine + asked)
-    start(given)
     lax.fori_loop(0, 4, prepare, 0)
 
     def group(g, _):

time: 91.7 us -> 91.1 us (level)
  no operation moved by 1% of the time
where the time goes in v8:
time: 91.1 us; the launch traced here: 90.4 us
  Pallas kernels  89.6 us (98%)
    pallas_call x1, Pallas kernels, shards(): pl.pallas_call(kernel, out_shape=shapes, in_specs=[pl.BlockSpec(memory_sp...  87.2 us
    pallas_call x1, Pallas kernels, shards(): pl.pallas_call(settle, out_shape=shapes, in_specs=[hbm] * 6, out_specs=[h...  2.36 us

profile of v8, /device:TPU:0, one launch (start us, length us, event | category | flops | bytes accessed | tf_op | source)
XLA Modules:
  0.0 90.4 jit_solution(12775372233354392155)
XLA Ops:
  0.6 87.2 %attention.1 = (bf16[2,128,1280]{2,1,0:T(8,128)(2,1)}, bf16[2,128,1280]{2,1,0:T(8,128)(2,1)}, bf16[2,128,256]{2,1,0:T(8,128)(2,1)}, bf16[2,128,256]{2,1,0:T(8,12...) custom-call(s32[2]{0:T(128)} %lens_ref.1, bf16[2,128,1280]{2,1,0:T(8,128)(2,1)} %queries.1, ...), custom_call_target="tpu_custom_call" | custom-call | tf_op jit(solution)/shard_map/attention/pallas_call | solution.py:456
  87.9 2.4 %settle.1 = (bf16[2,128,1280]{2,1,0:T(8,128)(2,1)}, bf16[2,128,1280]{2,1,0:T(8,128)(2,1)}, bf16[2,128,256]{2,1,0:T(8,128)(2,1)}, bf16[2,128,256]{2,1,0:T(8,128)(...) custom-call(bf16[2,128,1280]{2,1,0:T(8,128)(2,1)} %get-tuple-element.12.refs_0_, ...), custom_call_target="tpu_custom_call" | custom-call | tf_op jit(solution)/shard_map/settle/pallas_call | solution.py:475
